TPU v7x, 512 devices: a whole 4x4x16 slice. The times are simulated.
512 devices in a mesh: head: 64 (over x_lo, z, core), row: 8 (over y, x_hi).
Axes of the slice: x: 4 (x_hi: 2, x_lo: 2; x = x_hi * 2 + x_lo), y: 4, z: 16, core: 2. Of those that a mesh axis runs over, the one named last changes fastest.
Arguments:
- tokens: bfloat16 [2, 128, 4096], P(None, None, 'row'), may hold values from -6 to 6
- w_zx: bfloat16 [4096, 2, 8192], P('row', None, 'head'), may hold values from -0.09375 to 0.09375
- w_bc: bfloat16 [4096, 2048], P('row', 'head'), may hold values from -0.09375 to 0.09375
- w_dt: bfloat16 [4096, 128], P('row', 'head'), may hold values from -0.09375 to 0.09375
- conv_wx: float32 [4, 8192], P(None, 'head'), may hold values from -3 to 3
- conv_bx: float32 [8192], P('head'), may hold values from -3 to 3
- conv_wbc: float32 [4, 2048], P(None, 'head'), may hold values from -3 to 3
- conv_bbc: float32 [2048], P('head'), may hold values from -3 to 3
- dt_bias: float32 [128], P('head'), may hold values from -2 to 1
- decay_rate: float32 [128], P('head'), may hold values from 0.05 to 4
- skip_gain: float32 [128], P('head'), may hold values from 0.5 to 1.5
- norm_gain: float32 [8192], P('head'), may hold values from 0.5 to 1.5
- w_out: bfloat16 [8192, 4096], P('head', 'row'), may hold values from -0.0625 to 0.0625
- ssm_state: float32 [128, 128, 64, 128], P('row', 'head'), may hold values from -2 to 2
- tail_x: bfloat16 [128, 3, 8192], P('row', None, 'head'), may hold values from -6 to 6
- tail_bc: bfloat16 [128, 3, 2048], P('row', None, 'head'), may hold values from -6 to 6
Outputs:
- layer_out: bfloat16 [2, 128, 4096], P(None, 'head', 'row')
- state_out: float32 [128, 128, 64, 128], P('row', 'head')
- tail_x_out: bfloat16 [128, 3, 8192], P('row', None, 'head')
- tail_bc_out: bfloat16 [128, 3, 2048], P('row', None, 'head')
All inputs are finite; a program needn't handle non-finite values.
Results may differ from a plain program's by a relative error of at most 0.015.
Values may be sent and summed in bfloat16 or wider, within the bound.
A program may use at most 64 MiB of HBM per device.

v0:
```python
import jax
import jax.numpy as jnp
from jax import lax
from jax.sharding import PartitionSpec as P

H = 128
P_SIZE = 64
N = 128
G = 8
STEPS = 2


epsilon = 1e-05


def convolve(window, weight, offset):
    summed = jnp.sum(window.astype(jnp.float32) * weight[None, :, :], axis=1) + offset[None, :]
    return jax.nn.silu(summed).astype(jnp.bfloat16)


def local(
    tokens,
    w_zx,
    w_bc,
    w_dt,
    conv_wx,
    conv_bx,
    conv_wbc,
    conv_bbc,
    dt_bias,
    decay_rate,
    skip_gain,
    norm_gain,
    w_out,
    ssm_state,
    tail_x,
    tail_bc,
):
    head_count = lax.axis_size("head")
    heads_here = H // head_count
    width_here = heads_here * P_SIZE
    bc_here = w_bc.shape[1]
    local_rows = ssm_state.shape[0]
    feat_here = tokens.shape[2]
    columns = jnp.concatenate([w_zx.reshape(feat_here, 2 * width_here), w_bc, w_dt], axis=1)
    group_index = lax.axis_index("head") * heads_here // (H // G)
    selector = (jnp.arange(G) == group_index).astype(jnp.float32)
    neg_rate = -decay_rate
    projected = []
    for which_step in range(STEPS):
        project_block = tokens[which_step]
        projected.append(
            lax.psum_scatter(
                jnp.dot(project_block, columns, preferred_element_type=jnp.float32),
                "row",
                scatter_dimension=0,
                tiled=True,
            )
        )
    ssm_now = ssm_state
    outputs = []
    for which_step in range(STEPS):
        mixed = projected[which_step].astype(jnp.bfloat16)
        gate_raw = mixed[:, :width_here]
        x_raw = mixed[:, width_here : 2 * width_here]
        bc_raw = mixed[:, 2 * width_here : 2 * width_here + bc_here]
        dt_raw = mixed[:, 2 * width_here + bc_here :]
        window_x = jnp.concatenate([tail_x, x_raw[:, None, :]], axis=1)
        conv_x = convolve(window_x, conv_wx, conv_bx)
        tail_x = window_x[:, 1:, :]
        window_bc = jnp.concatenate([tail_bc, bc_raw[:, None, :]], axis=1)
        conv_bc = convolve(window_bc, conv_wbc, conv_bbc)
        tail_bc = window_bc[:, 1:, :]
        gathered = lax.all_gather(conv_bc, "head", axis=1, tiled=True)
        b_group = lax.dynamic_slice_in_dim(gathered, group_index * N, N, 1).astype(jnp.float32)
        c_group = lax.dynamic_slice_in_dim(gathered, (G + group_index) * N, N, 1).astype(
            jnp.float32
        )
        step_size = jax.nn.softplus(dt_raw.astype(jnp.float32) + dt_bias[None, :])
        decay_factor = jnp.exp(step_size * neg_rate[None, :])
        x_heads = conv_x.astype(jnp.float32).reshape(local_rows, heads_here, P_SIZE)
        ssm_now = (
            decay_factor[:, :, None, None] * ssm_now
            + (step_size[:, :, None] * x_heads)[:, :, :, None] * b_group[:, None, None, :]
        )
        y_heads = (
            jnp.einsum("rhpn,rn->rhp", ssm_now, c_group, precision=lax.Precision.HIGHEST)
            + skip_gain[None, :, None] * x_heads
        )
        gated = y_heads.reshape(local_rows, width_here) * jax.nn.silu(gate_raw.astype(jnp.float32))
        partial_sq = jnp.sum(gated * gated, axis=1)[:, None] * selector[None, :]
        totals = lax.psum(partial_sq, "head")
        mean_sq = jnp.sum(totals * selector[None, :], axis=1) / (H * P_SIZE // G)
        normed = (gated * lax.rsqrt(mean_sq + epsilon)[:, None] * norm_gain[None, :]).astype(
            jnp.bfloat16
        )
        gathered_rows = lax.all_gather(normed, "row", axis=0, tiled=True)
        outputs.append(
            lax.psum_scatter(
                jnp.dot(gathered_rows, w_out, preferred_element_type=jnp.float32),
                "head",
                scatter_dimension=0,
                tiled=True,
            ).astype(jnp.bfloat16)
        )
    layer_out = jnp.stack(outputs)
    return (layer_out, ssm_now, tail_x, tail_bc)


def solution(mesh):
    placed = (
        P(None, None, "row"),
        P("row", None, "head"),
        P("row", "head"),
        P("row", "head"),
        P(None, "head"),
        P("head"),
        P(None, "head"),
        P("head"),
        P("head"),
        P("head"),
        P("head"),
        P("head"),
        P("head", "row"),
        P("row", "head", None, None),
        P("row", None, "head"),
        P("row", None, "head"),
    )
    return jax.shard_map(
        local,
        mesh=mesh,
        in_specs=placed,
        out_specs=(
            P(None, "head", "row"),
            P("row", "head", None, None),
            P("row", None, "head"),
            P("row", None, "head"),
        ),
        check_vma=False,
    )
```

profile of v0, /device:TPU:1, one launch (start us, length us, event | category | flops | bytes accessed | tf_op | source)
XLA Modules:
  0.0 718.3 jit_solution(3326968802986295806)
XLA Ops:
  7.2 0.0 copy-start
  7.2 0.0 reduce-scatter.7.cloned.1.call-start
  7.2 0.9 copy.85
  8.2 0.2 copy.86
  8.4 0.0 copy-start.13
  8.5 0.9 copy-done.13
  9.4 0.3 convolution_bitcast_fusion.1
  9.7 0.8 copy.103
  10.5 0.0 reduce-scatter.7.cloned.1.call-update
  10.5 0.0 reduce-scatter.9.cloned.1.call-start
  10.6 0.3 convolution_bitcast_fusion
  10.9 0.8 copy.105
  11.7 0.0 reduce-scatter.9.cloned.1.call-update
  11.8 0.6 copy-done.14
  12.4 0.7 copy-done.15
  13.1 0.1 add.145
  13.2 1.3 dynamic-slice.4
  15.1 86.3 %reduce-scatter.7.cloned.1.call-done = f32[16,290]{1,0:T(8,128)} async-done(((f32[128,290]{1,0:T(8,128)}), f32[16,290]{1,0:T(8,128)}) %reduce-scatter.7.cloned.1.call-update) | async-done | bytes 18576 | tf_op jit(solution)/shard_map/reduce_scatter | solution.py:53
  101.4 0.7 convert_element_type.95
  102.2 87.8 %reduce-scatter.9.cloned.1.call-done = f32[16,290]{1,0:T(8,128)} async-done(((f32[128,290]{1,0:T(8,128)}), f32[16,290]{1,0:T(8,128)}) %reduce-scatter.9.cloned.1.call-update) | async-done | bytes 18576 | tf_op jit(solution)/shard_map/reduce_scatter | solution.py:53
  189.9 0.7 convert_element_type.107
  190.7 0.7 copy-done.4
  191.4 0.6 fusion.11
  192.0 0.1 copy-done.7
  192.1 0.1 reduce_sum.77
  192.2 0.6 copy-done.5
  192.8 0.6 fusion.10
  193.4 0.1 copy-done.8
  193.5 0.0 copy-start.9
  193.5 0.1 reduce_sum.82
  193.6 0.6 copy-done.9
  194.2 0.1 multiply_exponential_fusion
  194.3 0.1 copy.94
  194.3 0.1 copy.88
  194.4 0.1 convert_multiply_fusion.1
  194.5 0.0 copy-start.12
  194.5 0.6 copy-done.12
  195.2 66.6 %all-gather.1 = bf16[64,32,16]{1,2,0:T(8,128)(2,1)S(1)} all-gather(bf16[1,32,16]{1,2,0:T(8,128)(2,1)S(1)} %get-tuple-element.32), channel_id=1, replica_groups=mesh['head'=64,'row'=8] {'head'}, dimensions={0}, use_global_device_ids=true | all-gather | bytes 66560 | tf_op jit(solution)/shard_map/all_gather | solution.py:74
  261.8 0.1 copy.97
  261.9 0.3 reshape.99
  262.2 60.3 %all-gather = bf16[64,32,16]{1,2,0:T(8,128)(2,1)S(1)} all-gather(bf16[1,32,16]{1,2,0:T(8,128)(2,1)S(1)} %get-tuple-element.33), channel_id=1, replica_groups=mesh['head'=64,'row'=8] {'head'}, dimensions={0}, use_global_device_ids=true | all-gather | bytes 66560 | tf_op jit(solution)/shard_map/all_gather | solution.py:74
  322.5 0.1 copy.91
  322.5 0.3 reshape.97
  322.8 1.4 fusion
  324.3 0.8 multiply_add_fusion
  325.1 0.0 copy-start.1
  325.1 0.0 copy-start.10
  325.1 1.3 fusion.22
  326.4 0.1 fusion.9
  326.5 0.1 reshape.95
  326.6 0.1 multiply_reduce_fusion.4
  326.7 0.1 reshape.94
  326.8 0.1 multiply_reduce_fusion.5
  326.9 0.1 broadcast_multiply_fusion
  327.0 106.2 %all-reduce.3 = (f32[16,8]{0,1:T(8,128)S(1)}, f32[16,8]{0,1:T(8,128)S(1)}) all-reduce(f32[16,8]{0,1:T(8,128)S(1)} %get-tuple-element.31, f32[16,8]{0,1:T(8,128)S(1)} %get-tuple-element.30), channel_id=1, replica_groups=mesh['head'=64,'row'=8] {'head'}, use_global_device_ids=true, to_apply=%region_4.5 | all-reduce | flops 256 | bytes 2048 | tf_op jit(solution)/shard_map/psum | solution.py:92
  433.2 0.1 multiply_reduce_fusion.7
  433.3 0.6 copy-done.11
  434.0 0.1 multiply_convert_fusion.4
  434.1 27.8 %all_gather.13 = bf16[128,128]{1,0:T(8,128)(2,1)S(1)} all-gather(bf16[16,128]{1,0:T(8,128)(2,1)S(1)} %get-tuple-element.28), channel_id=1, replica_groups=mesh['head'=64,'row'=8] {'row'}, dimensions={0}, use_global_device_ids=true | all-gather | bytes 36864 | tf_op jit(solution)/shard_map/all_gather | solution.py:97
  461.8 27.7 %all_gather.15 = bf16[128,128]{1,0:T(8,128)(2,1)S(1)} all-gather(bf16[16,128]{1,0:T(8,128)(2,1)S(1)} %get-tuple-element.29), channel_id=1, replica_groups=mesh['head'=64,'row'=8] {'row'}, dimensions={0}, use_global_device_ids=true | all-gather | bytes 36864 | tf_op jit(solution)/shard_map/all_gather | solution.py:97
  489.6 0.2 fusion.32
  489.7 0.2 fusion.31
  489.9 220.9 %all-reduce.5 = (bf16[128,512]{1,0:T(8,128)(2,1)S(1)}, bf16[128,512]{1,0:T(8,128)(2,1)S(1)}) all-reduce(f32[128,512]{1,0:T(8,128)S(1)} %fusion.32, f32[128,512]{1,0:T(8,128)S(1)} %fusion.31), channel_id=5, replica_groups=mesh['head'=64,'row'=8] {'head'}, use_global_device_ids=true, to_apply=%region_13.14.clone | all-reduce | flops 131072 | bytes 786432
  710.8 0.6 pad_maximum_fusion.7
  (37 shorter events, 0.2 us)
Async XLA Ops:
  7.2 482.4 %copy-start = (bf16[128,512]{1,0:T(8,128)(2,1)S(1)}, bf16[128,512]{1,0:T(8,128)(2,1)}, u32[]{:S(2)}) copy-start(bf16[128,512]{1,0:T(8,128)(2,1)} %param.28) | copy-start | bytes 393220
  7.2 1.0 copy-start.6
  7.2 1.2 copy-start.3
  7.2 94.2 %reduce-scatter.7.cloned.1.call-start = ((), (), s32[]{:S(2)}) async-start(), calls=%async_computation.2 | async-start | bytes 221184 | tf_op jit(solution)/shard_map/reduce_scatter | solution.py:53
  8.4 1.0 copy-start.13
  10.5 179.4 %reduce-scatter.9.cloned.1.call-start = ((), (), s32[]{:S(2)}) async-start(), calls=%async_computation.3 | async-start | bytes 221184 | tf_op jit(solution)/shard_map/reduce_scatter | solution.py:53
  11.8 0.7 copy-start.14
  12.4 0.7 copy-start.15
  190.7 0.7 copy-start.4
  191.4 0.7 copy-start.7
  192.1 0.7 copy-start.5
  192.8 0.7 copy-start.8
  193.5 0.7 copy-start.9
  194.5 0.7 copy-start.12
  261.8 61.0 %copy-start.2 = (f32[16,2,64,128]{3,2,1,0:T(8,128)S(1)}, f32[16,2,64,128]{3,2,1,0:T(8,128)}, u32[]{:S(2)}) copy-start(f32[16,2,64,128]{3,2,1,0:T(8,128)} %param.29) | copy-start | bytes 3145732
  325.1 164.8 %copy-start.1 = (f32[16,2,64,128]{3,2,1,0:T(8,128)}, f32[16,2,64,128]{3,2,1,0:T(8,128)S(1)}, u32[]{:S(2)}) copy-start(f32[16,2,64,128]{3,2,1,0:T(8,128)S(1)} %multiply_add_fusion) | copy-start | bytes 3145732
  325.1 1.3 copy-start.10
  433.3 0.7 copy-start.11
Sparse Core Ops, SparseCore 0:
  13.0 88.3 reduce-scatter.6
  105.8 84.0 reduce-scatter.8
where the time goes:
time: 721 us; the launch traced here: 718 us
  blocking collectives  509 us (71%)
  waiting for transfers between devices  174 us (24%)
  between operations  15 us (2%)
  local copies, waits for them, and re-layouts  11 us (2%)
    unnamed x1, blocking collectives  221 us
    reduce_scatter x2, waiting for transfers between devices, local(): lax.psum_scatter(jnp.dot(project_block, columns, preferred_element_type=j...  174 us
    all_gather x2, blocking collectives, local(): gathered = lax.all_gather(conv_bc, 'head', axis=1, tiled=True)  127 us
    psum x1, blocking collectives, local(): totals = lax.psum(partial_sq, 'head')  106 us
    all_gather x2, blocking collectives, local(): gathered_rows = lax.all_gather(normed, 'row', axis=0, tiled=True)  55.5 us
  transfers between devices with their start and end apart: 2, of which 2 were waited for; matrix products, arithmetic and copies ran while one was open for 0% of the time, Pallas kernels for 0%

commit v1 on v0

v1 whole, which is shorter than its diff:
```python
import jax
import jax.numpy as jnp
from jax import lax
from jax.experimental import pallas as pl
from jax.experimental.pallas import tpu as pltpu
from jax.sharding import PartitionSpec as P

MESH = pl.DeviceIdType.MESH
F32 = jnp.float32
BF16 = jnp.bfloat16
EPS = 1e-05
NT = (((1,), (1,)), ((), ()))


def dot(a, b):
    return jnp.dot(a, b, preferred_element_type=F32)


def iota(shape, dim):
    return lax.broadcasted_iota(jnp.int32, shape, dim)


def kernel(
    tokens, w_zx, w_bc, w_dt, w_out, state,
    conv_wx, conv_bx, conv_wbc, conv_bbc, dt_bias, decay_rate, skip_gain, norm_gain, tail_x, tail_bc,
    layer_out, state_out, tail_x_out, tail_bc_out,
    tok, wz, wbc, wdt, st, zf, wa, wgx,
    sa, ra, sb, rb, sc, rc, s3, r3, r4, s5, r5, wo,
    tx, tb, gs, n4, f4, lhs, f5, o5, so,
    lsem, ssem, rsem, wsend, wrecv, csend, crecv, osem,
):
    row = lax.axis_index("row")
    head = lax.axis_index("head")
    grp = lax.div(head, 8)
    mem = lax.rem(head, 8)
    quart = lax.rem(head, 4)
    core = lax.rem(head, 2)
    owner_kind = lax.div(head, 32)
    bc_group = lax.div(lax.rem(head, 32), 4)

    loads = [
        pltpu.make_async_copy(src, dst, lsem.at[n])
        for n, (src, dst) in enumerate(
            ((tokens, tok), (w_bc, wbc), (w_dt, wdt), (w_zx, wz), (state, st))
        )
    ]
    for load in loads:
        load.start()

    barrier = pltpu.get_barrier_semaphore()

    def tell(h, r):
        pl.semaphore_signal(barrier, inc=1, device_id=(h, r), device_id_type=MESH)

    for d in range(1, 8):
        tell(head, lax.rem(row + d, 8))
    for d in range(1, 8):
        tell(grp * 8 + lax.rem(mem + d, 8), row)
    for d in range(1, 8):
        tell(lax.rem(head + 8 * d, 64), row)
    own_source = ((owner_kind == 0) & (grp == bc_group)) | ((owner_kind == 1) & (grp == bc_group))
    for n in range(8):
        src = (n // 4) * 32 + grp * 4 + n % 4

        @pl.when(src != head)
        def _():
            tell(src, row)

    lane = iota((16, 128), 1)
    loads[1].wait()
    spread = (iota((32, 128), 1) % 32 == iota((32, 128), 0)).astype(BF16)
    wa[:, :128] = dot(wbc[...], spread).astype(BF16)
    loads[2].wait()
    wd = wdt[...].astype(F32)
    wa[:, 128:] = jnp.where(iota((512, 128), 1) < 64, wd[:, 0:1], wd[:, 1:2]).astype(BF16)
    loads[0].wait()
    toks = tok[...].reshape(256, 512)
    pa = dot(toks, wa[...])
    for i in range(8):
        for s in range(2):
            sa[i, s * 16 : s * 16 + 16, :] = pa[s * 128 + i * 16 : s * 128 + i * 16 + 16, :128].astype(BF16)
            sb[i, 2, s * 16 : s * 16 + 16, :] = pa[s * 128 + i * 16 : s * 128 + i * 16 + 16, 128:].astype(BF16)

    pl.semaphore_wait(barrier, jnp.where(own_source, 28, 29))

    sends = []

    def send(src, dst, ss, rs, device):
        copy = pltpu.make_async_remote_copy(
            src_ref=src, dst_ref=dst, send_sem=ss, recv_sem=rs, device_id=device, device_id_type=MESH
        )
        copy.start()
        return copy

    for d in range(1, 8):
        to = lax.rem(row + d, 8)
        sends.append(send(sa.at[to], ra.at[row], ssem.at[0, d], rsem.at[0, row], (head, to)))

    loads[3].wait()
    zf[...] = wz[...].astype(F32)
    wgx[:, :128] = zf[pl.ds(0, 512, stride=2), :].astype(BF16)
    wgx[:, 128:] = zf[pl.ds(1, 512, stride=2), :].astype(BF16)
    pz = dot(toks, wgx[...])
    for i in range(8):
        for s in range(2):
            piece = pz[s * 128 + i * 16 : s * 128 + i * 16 + 16, :].astype(BF16)
            sb[i, 0, s * 16 : s * 16 + 16, :] = piece[:, :128]
            sb[i, 1, s * 16 : s * 16 + 16, :] = piece[:, 128:]
    for d in range(1, 8):
        to = lax.rem(row + d, 8)
        sends.append(send(sb.at[to], rb.at[row], ssem.at[1, d], rsem.at[1, row], (head, to)))

    for n in range(8):
        part = w_out.at[:, (n % 2) * 256 : (n % 2) * 256 + 256]
        place = wo.at[n % 2, pl.ds(mem * 128, 128), :]

        @pl.when(mem != n)
        def _():
            send(part, place, wsend.at[n], wrecv.at[mem], (grp * 8 + n, row))

        @pl.when(mem == n)
        def _():
            pltpu.make_async_copy(part, place, wrecv.at[mem]).start()

    ra[row] = sa[row]
    rb[row] = sb[row]

    tx[:, 0:3, :] = tail_x[...].astype(F32)
    narrow = tail_bc[...].astype(F32)
    tb[:, 0:3, :] = jnp.concatenate([narrow] * 4, axis=2)
    txr, tbr = tx.reshape(128, 128), tb.reshape(128, 128)

    def tail(ref, t):
        return ref[pl.ds(t, 16, stride=8), :]

    def windows(ref, raw, weight, bias):
        t0, t1, t2 = tail(ref, 0), tail(ref, 1), tail(ref, 2)
        r0, r1 = raw[:16], raw[16:]
        w = [weight[k : k + 1, :] for k in range(4)]
        c0 = t0 * w[0] + t1 * w[1] + t2 * w[2] + r0 * w[3] + bias
        c1 = t1 * w[0] + t2 * w[1] + r0 * w[2] + r1 * w[3] + bias
        both = jnp.concatenate([c0, c1], axis=0)
        return jax.nn.silu(both).astype(BF16)

    def new_tail(ref, raw):
        ref[pl.ds(0, 16, stride=8), :] = tail(ref, 2)
        ref[pl.ds(1, 16, stride=8), :] = raw[:16]
        ref[pl.ds(2, 16, stride=8), :] = raw[16:]

    weight_bc = jnp.concatenate([conv_wbc[...]] * 4, axis=1)
    bias_bc = jnp.concatenate([conv_bbc[...]] * 4, axis=1)

    def arrived(buf, sem):
        pltpu.make_async_copy(buf, buf, sem).wait()

    for d in range(1, 8):
        frm = lax.rem(row + d, 8)
        arrived(ra.at[frm], rsem.at[0, frm])
    total = ra[0].astype(F32)
    for i in range(1, 8):
        total += ra[i].astype(F32)
    raw_bc = total.astype(BF16).astype(F32)
    conv_bc = windows(tbr, raw_bc, weight_bc, bias_bc).astype(F32)
    sc[...] = jnp.where(lax.div(iota((32, 128), 1), 32) == quart, conv_bc, 0.0).astype(BF16)
    slot = owner_kind * 4 + quart
    for n in range(8):
        to = bc_group * 8 + n

        @pl.when(to != head)
        def _():
            send(sc, rc.at[slot], ssem.at[2, n], rsem.at[2, slot], (to, row))

        @pl.when(to == head)
        def _():
            pltpu.make_async_copy(sc, rc.at[slot], rsem.at[2, slot]).start()

    new_tail(tbr, raw_bc)
    tail_bc_out[...] = tb[:, 0:3, 0:32].astype(BF16)

    for d in range(1, 8):
        frm = lax.rem(row + d, 8)
        arrived(rb.at[frm], rsem.at[1, frm])
    mixed = []
    for part in range(3):
        total = rb[0, part].astype(F32)
        for i in range(1, 8):
            total += rb[i, part].astype(F32)
        mixed.append(total.astype(BF16).astype(F32))
    gate_raw, raw_x, dt_raw = mixed
    xc = windows(txr, raw_x, conv_wx[...], conv_bx[...]).astype(F32)
    new_tail(txr, raw_x)
    tail_x_out[...] = tx[:, 0:3, :].astype(BF16)
    first = iota((1, 128), 1) < 64

    def per_head(ref):
        return jnp.where(first, ref[0], ref[1])

    step_size = jax.nn.softplus(dt_raw + per_head(dt_bias))
    decay = jnp.exp(-step_size * per_head(decay_rate))
    a = step_size * xc
    skip = per_head(skip_gain) * xc
    gate = jax.nn.silu(gate_raw)
    d0, d1 = decay[:16], decay[16:]
    d01 = d0 * d1
    a0, a1 = a[:16], a[16:]
    loads[4].wait()

    for n in range(8):
        arrived(rc.at[n], rsem.at[2, n])
    b = rc[0].astype(F32) + rc[1].astype(F32) + rc[2].astype(F32) + rc[3].astype(F32)
    c = rc[4].astype(F32) + rc[5].astype(F32) + rc[6].astype(F32) + rc[7].astype(F32)
    c_low = c.astype(BF16)
    b0, b1 = b[:16], b[16:]
    c0, c1 = c[:16], c[16:]
    mod16 = iota((32, 128), 0) % 16
    read = jnp.zeros((32, 128), F32)
    for r in range(16):
        one = lax.dot_general(c_low, st[r].astype(BF16), NT, preferred_element_type=F32)
        read = jnp.where(mod16 == r, one, read)

    def along(u, v):
        return jnp.sum(u * v, axis=1, keepdims=True)

    y0 = d0 * read[:16] + a0 * along(b0, c0)
    y1 = d01 * read[16:] + d1 * a0 * along(b0, c1) + a1 * along(b1, c1)
    gated = (jnp.concatenate([y0, y1], axis=0) + skip) * gate
    gs[...] = gated
    s3[...] = jnp.zeros_like(s3)
    s3r = s3.reshape(64, 128)
    for s in range(2):
        for k in range(2):
            s3r[pl.ds(s * 2 + k, 8, stride=8), :] = gs[pl.ds(s * 16 + k, 8, stride=2), :]
    s3r[pl.ds(4, 8, stride=8), :] = jnp.broadcast_to(norm_gain[...], (8, 128))

    for d in range(1, 8):
        to = lax.rem(mem + d, 8)
        sends.append(send(s3.at[to], r3.at[mem], ssem.at[3, d], rsem.at[3, mem], (grp * 8 + to, row)))
    r3[mem] = s3[mem]

    def high_low(v):
        high = v.astype(BF16).astype(F32)
        return [high, (v - high).astype(BF16).astype(F32)]

    d10 = d1 * a0
    zero = jnp.zeros((16, 128), F32)
    columns = jnp.concatenate(
        high_low(d01) + high_low(d10) + high_low(a1) + [zero, zero], axis=0
    )
    columns = jnp.transpose(columns).astype(BF16)
    one = jnp.ones((16, 128), F32)
    left = jnp.concatenate([zero, zero, b0, b0, b1, b1, zero, zero], axis=0)
    right = jnp.concatenate([one, one, zero, zero, zero, zero, zero, zero], axis=0)
    both = jnp.concatenate([left, right], axis=1)
    which = iota((128, 256), 0) % 16

    def update(r):
        picked = jnp.where(which == r, both, 0.0).astype(BF16)
        made = dot(columns, picked)
        so[r] = st[r] * made[:, 128:] + made[:, :128]

    for r in range(8):
        update(r)

    for d in range(1, 8):
        frm = lax.rem(mem + d, 8)
        arrived(r3.at[frm], rsem.at[3, frm])
    square = jnp.zeros((8, 128), F32)
    for n in range(8):
        square += r3[n] * r3[n]
    scale = lax.rsqrt(jnp.sum(square, axis=1, keepdims=True) / 1024.0 + EPS)
    for n in range(8):
        block = r3[n]
        n4[n * 4 : n * 4 + 4, :] = (block * scale * block[4:5, :])[:4]
    r4[row] = n4[...].astype(BF16)
    for d in range(1, 8):
        to = lax.rem(row + d, 8)
        sends.append(send(r4.at[row], r4.at[row], ssem.at[4, d], rsem.at[4, row], (head, to)))

    for n in range(8):
        arrived(wo.at[core, pl.ds(n * 128, 128), :], wrecv.at[n])
    sibling = head + 1 - 2 * core
    sends.append(send(wo.at[core], wo.at[core], csend, crecv, (sibling, row)))

    for r in range(8, 16):
        update(r)
    write = pltpu.make_async_copy(so, state_out, osem)
    write.start()

    for d in range(1, 8):
        frm = lax.rem(row + d, 8)
        arrived(r4.at[frm], rsem.at[4, frm])
    f4[...] = r4[...].reshape(256, 128).astype(F32)
    for n in range(8):
        block = [f4[pl.ds(n * 4 + rr, 8, stride=32), :] for rr in range(4)]
        lhs[:, n * 128 : n * 128 + 128] = jnp.concatenate(block, axis=0).astype(BF16)
    arrived(wo.at[1 - core], crecv)
    f5r = f5.reshape(128, 128)
    for half in range(2):
        out = dot(lhs[...], wo[half])
        for rr in range(4):
            for k in range(2):
                f5r[pl.ds(rr * 4 + half * 2 + k, 8, stride=16), :] = out[rr * 8 : rr * 8 + 8, k * 128 : k * 128 + 128]
    s5[...] = f5[...].astype(BF16)
    for d in range(1, 8):
        to = lax.rem(grp + d, 8)
        sends.append(send(s5.at[to], r5.at[grp], ssem.at[5, d], rsem.at[5, grp], (to * 8 + mem, row)))
    r5[grp] = s5[grp]
    for d in range(1, 8):
        frm = lax.rem(grp + d, 8)
        arrived(r5.at[frm], rsem.at[5, frm])
    total = r5[0].astype(F32)
    for i in range(1, 8):
        total += r5[i].astype(F32)
    o5[...] = total
    for s in range(2):
        for k in range(4):
            pair = o5[pl.ds(s * 8 + k, 2, stride=4), :]
            layer_out[s, :, k * 128 : k * 128 + 128] = pair.astype(BF16)

    for copy in sends:
        copy.wait_send()
    for n in range(8):

        @pl.when(mem != n)
        def _():
            arrived(w_out.at[:, 0:256], wsend.at[n])

        @pl.when(bc_group * 8 + n != head)
        def _():
            arrived(sc, ssem.at[2, n])

    write.wait()


def local(
    tokens, w_zx, w_bc, w_dt, conv_wx, conv_bx, conv_wbc, conv_bbc,
    dt_bias, decay_rate, skip_gain, norm_gain, w_out, ssm_state, tail_x, tail_bc,
):
    hbm = pl.BlockSpec(memory_space=pl.ANY)
    vmem = pl.BlockSpec(memory_space=pltpu.VMEM)
    smem = pl.BlockSpec(memory_space=pltpu.SMEM)
    V = pltpu.VMEM
    dma = pltpu.SemaphoreType.DMA
    outs = pl.pallas_call(
        kernel,
        out_shape=(
            jax.ShapeDtypeStruct((2, 2, 512), BF16),
            jax.ShapeDtypeStruct((16, 128, 128), F32),
            jax.ShapeDtypeStruct((16, 3, 128), BF16),
            jax.ShapeDtypeStruct((16, 3, 32), BF16),
        ),
        in_specs=[hbm] * 6 + [vmem] * 4 + [smem] * 3 + [vmem] * 3,
        out_specs=(vmem, hbm, vmem, vmem),
        scratch_shapes=[
            V((2, 128, 512), BF16),
            V((1024, 128), BF16),
            V((512, 32), BF16),
            V((512, 2), BF16),
            V((16, 128, 128), F32),
            V((1024, 128), F32),
            V((512, 256), BF16),
            V((512, 256), BF16),
            V((8, 32, 128), BF16),
            V((8, 32, 128), BF16),
            V((8, 3, 32, 128), BF16),
            V((8, 3, 32, 128), BF16),
            V((32, 128), BF16),
            V((8, 32, 128), BF16),
            V((8, 8, 128), F32),
            V((8, 8, 128), F32),
            V((8, 32, 128), BF16),
            V((8, 16, 128), BF16),
            V((8, 16, 128), BF16),
            V((2, 1024, 256), BF16),
            V((16, 8, 128), F32),
            V((16, 8, 128), F32),
            V((32, 128), F32),
            V((32, 128), F32),
            V((256, 128), F32),
            V((32, 1024), BF16),
            V((8, 16, 128), F32),
            V((16, 128), F32),
            V((16, 128, 128), F32),
            dma((5,)),
            dma((6, 8)),
            dma((6, 8)),
            dma((8,)),
            dma((8,)),
            dma,
            dma,
            dma,
        ],
        compiler_params=pltpu.CompilerParams(
            collective_id=0, has_side_effects=True, vmem_limit_bytes=40 << 20
        ),
    )(
        tokens,
        w_zx.reshape(1024, 128),
        w_bc,
        w_dt,
        w_out,
        ssm_state.reshape(16, 128, 128),
        conv_wx,
        conv_bx.reshape(1, 128),
        conv_wbc,
        conv_bbc.reshape(1, 32),
        dt_bias,
        decay_rate,
        skip_gain,
        norm_gain.reshape(1, 128),
        tail_x,
        tail_bc,
    )
    return outs[0], outs[1].reshape(16, 2, 64, 128), outs[2], outs[3]


def solution(mesh):
    placed = (
        P(None, None, "row"),
        P("row", None, "head"),
        P("row", "head"),
        P("row", "head"),
        P(None, "head"),
        P("head"),
        P(None, "head"),
        P("head"),
        P("head"),
        P("head"),
        P("head"),
        P("head"),
        P("head", "row"),
        P("row", "head", None, None),
        P("row", None, "head"),
        P("row", None, "head"),
    )
    return jax.shard_map(
        local,
        mesh=mesh,
        in_specs=placed,
        out_specs=(
            P(None, "head", "row"),
            P("row", "head", None, None),
            P("row", None, "head"),
            P("row", None, "head"),
        ),
        check_vma=False,
    )
```

time: 721 us -> 65.8 us (0.09)
  blocking collectives: 509 us -> 0 us
  waiting for transfers between devices: 174 us -> 0 us
  Pallas kernels: 0 us -> 56 us
  between operations: 15 us -> 0.81 us
    unnamed x1 -> x0, blocking collectives: 221 us -> none
    all_gather x4 -> x0, blocking collectives: 182 us -> none  [the longest x2 127 us: local(): gathered = lax.all_gather(conv_bc, 'head', axis=1, tiled=True)]
    reduce_scatter x2 -> x0, waiting for transfers between devices: 174 us -> none  [local(): lax.psum_scatter(jnp.dot(project_block, columns, preferred_element_type=j...]
    psum x1 -> x0, blocking collectives: 106 us -> none  [local(): totals = lax.psum(partial_sq, 'head')]
    pallas_call x0 -> x1, Pallas kernels: none -> 56 us  [local(): pl.pallas_call(kernel, out_shape=(jax.ShapeDtypeStruct((2, 2, 512), BF16)...]
  transfers between devices with their start and end apart: 2 -> 0, of which waited for: 2 -> 0; matrix products, arithmetic and copies ran while one was open for 0% -> 0% of each run, Pallas kernels for 0% -> 0%
where the time goes in v1:
time: 65.8 us; the launch traced here: 65.2 us
  Pallas kernels  56 us (85%)
  local copies, waits for them, and re-layouts  8.38 us (13%)
  between operations  0.81 us (1%)
    pallas_call x1, Pallas kernels, local(): pl.pallas_call(kernel, out_shape=(jax.ShapeDtypeStruct((2, 2, 512), BF16)...  56 us
    unnamed x34, local copies, waits for them, and re-layouts  8.38 us

profile of v1, /device:TPU:1, one launch (start us, length us, event | category | flops | bytes accessed | tf_op | source)
XLA Modules:
  0.0 65.2 jit_solution(8901435569186805681)
XLA Ops:
  0.6 0.0 copy-start.12
  0.6 0.0 copy-start.1
  0.7 0.8 %copy.22.tail_x = bf16[16,3,128]{2,1,0:T(4,128)(2,1)S(1)} copy(bf16[16,3,128]{2,0,1:T(8,128)(2,1)} %param.30) | data formatting | bytes 24576 | tf_op args[14]
  1.4 0.7 %copy.23.tail_bc = bf16[16,3,32]{2,1,0:T(4,128)(2,1)S(1)} copy(bf16[16,3,32]{2,0,1:T(8,128)(2,1)} %param.31) | data formatting | bytes 6144 | tf_op args[15]
  2.1 0.0 copy-done.12
  2.1 0.1 copy.20.w_bc
  2.3 0.0 copy-start.4
  2.3 0.0 copy-start.5
  2.3 0.0 copy-start.6
  2.3 0.0 copy-start.7
  2.3 0.0 copy-start.8
  2.3 0.0 copy-start.9
  2.3 0.0 copy-start.10
  2.3 0.0 copy-start.11
  2.3 0.9 %copy.21.w_dt = bf16[512,2]{1,0:T(8,128)(2,1)S(1)} copy(bf16[512,2]{0,1:T(2,128)(2,1)} %param.19) | data formatting | bytes 4096 | tf_op args[3]
  3.2 0.0 copy-done.1
  3.3 0.0 copy-done.4
  3.3 0.0 copy-done.5
  3.3 0.0 copy-done.6
  3.3 0.0 copy-done.7
  3.3 0.0 copy-done.8
  3.3 0.0 copy-done.9
  3.3 0.0 copy-done.10
  3.3 0.0 copy-done.11
  3.3 0.0 copy-start
  3.3 1.2 %copy-done = f32[16,2,64,128]{3,2,1,0:T(8,128)S(1)} copy-done((f32[16,2,64,128]{3,2,1,0:T(8,128)S(1)}, f32[16,2,64,128]{3,2,1,0:T(8,128)}, u32[]{:S(2)}) %copy-start) | copy-done | bytes 1048600
  4.6 0.0 copy-start.2
  4.6 0.9 %copy-done.2 = bf16[512,2,128]{2,1,0:T(2,128)(2,1)S(1)} copy-done((bf16[512,2,128]{2,1,0:T(2,128)(2,1)S(1)}, bf16[512,2,128]{2,1,0:T(2,128)(2,1)}, u32[]{:S(2)}) %copy-start.2) | copy-done | bytes 262168
  5.5 0.0 copy-start.3
  5.5 0.9 %copy-done.3 = bf16[128,512]{1,0:T(8,128)(2,1)S(1)} copy-done((bf16[128,512]{1,0:T(8,128)(2,1)S(1)}, bf16[128,512]{1,0:T(8,128)(2,1)}, u32[]{:S(2)}) %copy-start.3) | copy-done | bytes 131096
  6.4 56.0 %shard_map.183 = (bf16[2,2,512]{2,1,0:T(2,128)(2,1)S(1)}, f32[16,128,128]{2,1,0:T(8,128)S(1)}, bf16[16,3,128]{2,1,0:T(4,128)(2,1)S(1)}, bf16[16,3,32]{2,1,0:T(4,128)(2,1)S(1)}) custom-call(bf16[2,128,512]{2,1,0:T(8,128)(2,1)S(1)} %copy-done.1, bf16[1024,128]{1,0:T(8,128)(2,1)S(1)} %bitcast.8, bf16[512,32]{1,0:T(8,128)(2,1)S(1)} %copy.20.w_bc, ...), custom_call_target="tpu_custom_call" | custom-call | tf_op jit(solution)/shard_map/pallas_call | solution.py:344
  62.4 0.6 copy.24
  63.0 0.6 copy.25
  63.6 0.6 copy.28
  64.2 1.0 %copy.29 = f32[16,2,64,128]{3,2,1,0:T(8,128)} copy(f32[16,2,64,128]{3,2,1,0:T(8,128)S(1)} %bitcast.7) | data formatting | bytes 2097152
Async XLA Ops:
  0.6 1.5 %copy-start.12 = (bf16[512,32]{0,1:T(8,128)(2,1)S(1)}, bf16[512,32]{0,1:T(8,128)(2,1)}, u32[]{:S(2)}) copy-start(bf16[512,32]{0,1:T(8,128)(2,1)} %param.18) | copy-start | bytes 98308
  0.6 2.6 %copy-start.1 = (bf16[2,128,512]{2,1,0:T(8,128)(2,1)S(1)}, bf16[2,128,512]{2,1,0:T(8,128)(2,1)}, u32[]{:S(2)}) copy-start(bf16[2,128,512]{2,1,0:T(8,128)(2,1)} %tokens.1) | copy-start | bytes 786436
  2.3 1.0 %copy-start.4 = (f32[4,128]{1,0:T(4,128)S(1)}, f32[4,128]{1,0:T(4,128)}, u32[]{:S(2)}) copy-start(f32[4,128]{1,0:T(4,128)} %conv_wx.1) | copy-start | bytes 6148
  2.3 1.0 %copy-start.5 = (f32[4,32]{1,0:T(4,128)S(1)}, f32[4,32]{1,0:T(4,128)}, u32[]{:S(2)}) copy-start(f32[4,32]{1,0:T(4,128)} %conv_wbc.1) | copy-start | bytes 1540
  2.3 1.0 %copy-start.6 = (f32[128]{0:T(128)S(1)}, f32[128]{0:T(128)}, u32[]{:S(2)}) copy-start(f32[128]{0:T(128)} %param.21) | copy-start | bytes 1540
  2.3 1.0 %copy-start.7 = (f32[32]{0:T(128)S(1)}, f32[32]{0:T(128)}, u32[]{:S(2)}) copy-start(f32[32]{0:T(128)} %param.23) | copy-start | bytes 388
  2.3 1.0 %copy-start.8 = (f32[2]{0:T(128)S(1)}, f32[2]{0:T(128)}, u32[]{:S(2)}) copy-start(f32[2]{0:T(128)} %dt_bias.1) | copy-start | bytes 28
  2.3 1.0 %copy-start.9 = (f32[2]{0:T(128)S(1)}, f32[2]{0:T(128)}, u32[]{:S(2)}) copy-start(f32[2]{0:T(128)} %decay_rate.1) | copy-start | bytes 28
  2.3 1.0 %copy-start.10 = (f32[2]{0:T(128)S(1)}, f32[2]{0:T(128)}, u32[]{:S(2)}) copy-start(f32[2]{0:T(128)} %skip_gain.1) | copy-start | bytes 28
  2.3 1.0 %copy-start.11 = (f32[128]{0:T(128)S(1)}, f32[128]{0:T(128)}, u32[]{:S(2)}) copy-start(f32[128]{0:T(128)} %param.27) | copy-start | bytes 1540
  3.3 1.2 %copy-start = (f32[16,2,64,128]{3,2,1,0:T(8,128)S(1)}, f32[16,2,64,128]{3,2,1,0:T(8,128)}, u32[]{:S(2)}) copy-start(f32[16,2,64,128]{3,2,1,0:T(8,128)} %param.29) | copy-start | bytes 3145732
  4.6 0.9 %copy-start.2 = (bf16[512,2,128]{2,1,0:T(2,128)(2,1)S(1)}, bf16[512,2,128]{2,1,0:T(2,128)(2,1)}, u32[]{:S(2)}) copy-start(bf16[512,2,128]{2,1,0:T(2,128)(2,1)} %param.17) | copy-start | bytes 786436
  5.5 0.9 %copy-start.3 = (bf16[128,512]{1,0:T(8,128)(2,1)S(1)}, bf16[128,512]{1,0:T(8,128)(2,1)}, u32[]{:S(2)}) copy-start(bf16[128,512]{1,0:T(8,128)(2,1)} %w_out.1) | copy-start | bytes 393220

commit v2 on v1

--- a/solution.py
+++ b/solution.py
@@ -21,13 +21,14 @@
 
 
 def kernel(
-    tokens, w_zx, w_bc, w_dt, w_out, state,
-    conv_wx, conv_bx, conv_wbc, conv_bbc, dt_bias, decay_rate, skip_gain, norm_gain, tail_x, tail_bc,
-    layer_out, state_out, tail_x_out, tail_bc_out,
-    tok, wz, wbc, wdt, st, zf, wa, wgx,
+    tokens_h, w_zx_h, w_bc_h, w_dt_h, w_out, state_h,
+    conv_wx_h, conv_bx_h, conv_wbc_h, conv_bbc_h, dt_bias_h, decay_rate_h, skip_gain_h, norm_gain_h, tail_x_h, tail_bc_h,
+    layer_out, so, tail_x_out, tail_bc_out,
+    tok, wz, wbc, wdt, st, conv_wx, conv_bx, conv_wbc, conv_bbc, dt_bias, decay_rate, skip_gain, norm_gain, tail_x, tail_bc,
+    zf, wa, wgx,
     sa, ra, sb, rb, sc, rc, s3, r3, r4, s5, r5, wo,
-    tx, tb, gs, n4, f4, lhs, f5, o5, so,
-    lsem, ssem, rsem, wsend, wrecv, csend, crecv, osem,
+    gs, n4, f4, lhs, f5, o5,
+    lsem, ssem, rsem, wsend, wrecv, csend, crecv, near, far,
 ):
     row = lax.axis_index("row")
     head = lax.axis_index("head")
@@ -38,53 +39,67 @@
     owner_kind = lax.div(head, 32)
     bc_group = lax.div(lax.rem(head, 32), 4)
 
-    loads = [
-        pltpu.make_async_copy(src, dst, lsem.at[n])
-        for n, (src, dst) in enumerate(
-            ((tokens, tok), (w_bc, wbc), (w_dt, wdt), (w_zx, wz), (state, st))
-        )
-    ]
+    barrier = pltpu.get_barrier_semaphore()
+
+    def signal(sem, h, r):
+        pl.semaphore_signal(sem, inc=1, device_id=(h, r), device_id_type=MESH)
+
+    chip = head - core
+    for d in range(1, 8):
+        signal(barrier, chip, lax.rem(row + d, 8))
+    for d in range(1, 4):
+        signal(barrier, grp * 8 + lax.rem(mem - core + 2 * d, 8), row)
+
+    @pl.when(core == 1)
+    def _():
+        signal(barrier, chip, row)
+
+    for d in range(1, 8):
+        signal(barrier, lax.rem(chip + 8 * d, 64) + 1, row)
+    for n in range(4):
+        src = (n // 2) * 32 + grp * 4 + (n % 2) * 2
+
+        @pl.when(src != chip)
+        def _():
+            signal(barrier, src + 1, row)
+
+    sources = (
+        tokens_h, w_bc_h, w_dt_h, w_zx_h, state_h, conv_wbc_h, conv_bbc_h, tail_bc_h,
+        conv_wx_h, conv_bx_h, dt_bias_h, decay_rate_h, skip_gain_h, norm_gain_h, tail_x_h,
+    )
+    targets = (
+        tok, wbc, wdt, wz, st, conv_wbc, conv_bbc, tail_bc,
+        conv_wx, conv_bx, dt_bias, decay_rate, skip_gain, norm_gain, tail_x,
+    )
+    loads = [pltpu.make_async_copy(a, b, lsem.at[n]) for n, (a, b) in enumerate(zip(sources, targets))]
     for load in loads:
         load.start()
 
-    barrier = pltpu.get_barrier_semaphore()
-
-    def tell(h, r):
-        pl.semaphore_signal(barrier, inc=1, device_id=(h, r), device_id_type=MESH)
-
-    for d in range(1, 8):
-        tell(head, lax.rem(row + d, 8))
-    for d in range(1, 8):
-        tell(grp * 8 + lax.rem(mem + d, 8), row)
-    for d in range(1, 8):
-        tell(lax.rem(head + 8 * d, 64), row)
-    own_source = ((owner_kind == 0) & (grp == bc_group)) | ((owner_kind == 1) & (grp == bc_group))
-    for n in range(8):
-        src = (n // 4) * 32 + grp * 4 + n % 4
-
-        @pl.when(src != head)
-        def _():
-            tell(src, row)
-
-    lane = iota((16, 128), 1)
     loads[1].wait()
-    spread = (iota((32, 128), 1) % 32 == iota((32, 128), 0)).astype(BF16)
-    wa[:, :128] = dot(wbc[...], spread).astype(BF16)
+    for n in range(4):
+        wa[n * 32 : n * 32 + 32, :] = wbc[...]
     loads[2].wait()
     wd = wdt[...].astype(F32)
-    wa[:, 128:] = jnp.where(iota((512, 128), 1) < 64, wd[:, 0:1], wd[:, 1:2]).astype(BF16)
+    wa[128:, :] = jnp.where(iota((128, 512), 0) < 64, wd[0:1], wd[1:2]).astype(BF16)
     loads[0].wait()
     toks = tok[...].reshape(256, 512)
-    pa = dot(toks, wa[...])
+    pa = lax.dot_general(toks, wa[...], NT, preferred_element_type=F32)
     for i in range(8):
         for s in range(2):
             sa[i, s * 16 : s * 16 + 16, :] = pa[s * 128 + i * 16 : s * 128 + i * 16 + 16, :128].astype(BF16)
             sb[i, 2, s * 16 : s * 16 + 16, :] = pa[s * 128 + i * 16 : s * 128 + i * 16 + 16, 128:].astype(BF16)
 
-    pl.semaphore_wait(barrier, jnp.where(own_source, 28, 29))
+    @pl.when(core == 0)
+    def _():
+        pl.semaphore_wait(barrier, 21)
+        signal(near, head + 1, row)
+
+    @pl.when(core == 1)
+    def _():
+        pl.semaphore_wait(near, 1)
+
 
     sends = []
-
     def send(src, dst, ss, rs, device):
         copy = pltpu.make_async_remote_copy(
             src_ref=src, dst_ref=dst, send_sem=ss, recv_sem=rs, device_id=device, device_id_type=MESH
@@ -125,16 +140,11 @@
     ra[row] = sa[row]
     rb[row] = sb[row]
 
-    tx[:, 0:3, :] = tail_x[...].astype(F32)
-    narrow = tail_bc[...].astype(F32)
-    tb[:, 0:3, :] = jnp.concatenate([narrow] * 4, axis=2)
-    txr, tbr = tx.reshape(128, 128), tb.reshape(128, 128)
-
-    def tail(ref, t):
-        return ref[pl.ds(t, 16, stride=8), :]
-
-    def windows(ref, raw, weight, bias):
-        t0, t1, t2 = tail(ref, 0), tail(ref, 1), tail(ref, 2)
+    for n in range(5, 15):
+        loads[n].wait()
+
+    def windows(t, raw, weight, bias):
+        t0, t1, t2 = t
         r0, r1 = raw[:16], raw[16:]
         w = [weight[k : k + 1, :] for k in range(4)]
         c0 = t0 * w[0] + t1 * w[1] + t2 * w[2] + r0 * w[3] + bias
@@ -142,11 +152,14 @@
         both = jnp.concatenate([c0, c1], axis=0)
         return jax.nn.silu(both).astype(BF16)
 
-    def new_tail(ref, raw):
-        ref[pl.ds(0, 16, stride=8), :] = tail(ref, 2)
-        ref[pl.ds(1, 16, stride=8), :] = raw[:16]
-        ref[pl.ds(2, 16, stride=8), :] = raw[16:]
-
+    def new_tail(ref, old, raw):
+        width = ref.shape[2]
+        ref[0] = old[2]
+        ref[1] = raw[:16, :width].astype(BF16)
+        ref[2] = raw[16:, :width].astype(BF16)
+
+    old_bc = [jnp.concatenate([tail_bc[k].astype(F32)] * 4, axis=1) for k in range(3)]
+    old_x = [tail_x[k].astype(F32) for k in range(3)]
     weight_bc = jnp.concatenate([conv_wbc[...]] * 4, axis=1)
     bias_bc = jnp.concatenate([conv_bbc[...]] * 4, axis=1)
 
@@ -160,8 +173,18 @@
     for i in range(1, 8):
         total += ra[i].astype(F32)
     raw_bc = total.astype(BF16).astype(F32)
-    conv_bc = windows(tbr, raw_bc, weight_bc, bias_bc).astype(F32)
+    conv_bc = windows(old_bc, raw_bc, weight_bc, bias_bc).astype(F32)
     sc[...] = jnp.where(lax.div(iota((32, 128), 1), 32) == quart, conv_bc, 0.0).astype(BF16)
+
+    @pl.when(core == 1)
+    def _():
+        pl.semaphore_wait(barrier, jnp.where(grp == bc_group, 20, 22))
+        signal(far, head - 1, row)
+
+    @pl.when(core == 0)
+    def _():
+        pl.semaphore_wait(far, 1)
+
     slot = owner_kind * 4 + quart
     for n in range(8):
         to = bc_group * 8 + n
@@ -174,8 +197,7 @@
         def _():
             pltpu.make_async_copy(sc, rc.at[slot], rsem.at[2, slot]).start()
 
-    new_tail(tbr, raw_bc)
-    tail_bc_out[...] = tb[:, 0:3, 0:32].astype(BF16)
+    new_tail(tail_bc_out, tail_bc, raw_bc)
 
     for d in range(1, 8):
         frm = lax.rem(row + d, 8)
@@ -187,13 +209,12 @@
             total += rb[i, part].astype(F32)
         mixed.append(total.astype(BF16).astype(F32))
     gate_raw, raw_x, dt_raw = mixed
-    xc = windows(txr, raw_x, conv_wx[...], conv_bx[...]).astype(F32)
-    new_tail(txr, raw_x)
-    tail_x_out[...] = tx[:, 0:3, :].astype(BF16)
+    xc = windows(old_x, raw_x, conv_wx[...], conv_bx[...]).astype(F32)
+    new_tail(tail_x_out, tail_x, raw_x)
     first = iota((1, 128), 1) < 64
 
     def per_head(ref):
-        return jnp.where(first, ref[0], ref[1])
+        return jnp.where(first, ref[:, 0:1], ref[:, 1:2])
 
     step_size = jax.nn.softplus(dt_raw + per_head(dt_bias))
     decay = jnp.exp(-step_size * per_head(decay_rate))
@@ -283,8 +304,6 @@
 
     for r in range(8, 16):
         update(r)
-    write = pltpu.make_async_copy(so, state_out, osem)
-    write.start()
 
     for d in range(1, 8):
         frm = lax.rem(row + d, 8)
@@ -329,36 +348,73 @@
         def _():
             arrived(sc, ssem.at[2, n])
 
-    write.wait()
+
+def hand_over(a, b, c, d, oa, ob, oc, od, sem):
+    copies = [
+        pltpu.make_async_copy(src, dst, sem.at[n])
+        for n, (src, dst) in enumerate(((a, oa), (b, ob), (c, oc), (d, od)))
+    ]
+    for copy in copies:
+        copy.start()
+    for copy in copies:
+        copy.wait()
 
 
 def local(
     tokens, w_zx, w_bc, w_dt, conv_wx, conv_bx, conv_wbc, conv_bbc,
     dt_bias, decay_rate, skip_gain, norm_gain, w_out, ssm_state, tail_x, tail_bc,
 ):
-    hbm = pl.BlockSpec(memory_space=pl.ANY)
+    hbm = pl.BlockSpec(memory_space=pltpu.HBM)
     vmem = pl.BlockSpec(memory_space=pltpu.VMEM)
-    smem = pl.BlockSpec(memory_space=pltpu.SMEM)
     V = pltpu.VMEM
     dma = pltpu.SemaphoreType.DMA
-    outs = pl.pallas_call(
+    shapes = (
+        jax.ShapeDtypeStruct((2, 2, 512), BF16),
+        jax.ShapeDtypeStruct((16, 128, 128), F32),
+        jax.ShapeDtypeStruct((3, 16, 128), BF16),
+        jax.ShapeDtypeStruct((3, 16, 32), BF16),
+    )
+    operands = (
+        tokens,
+        w_zx.reshape(1024, 128),
+        w_bc.T,
+        w_dt.T,
+        w_out,
+        ssm_state.reshape(16, 128, 128),
+        conv_wx,
+        conv_bx.reshape(1, 128),
+        conv_wbc,
+        conv_bbc.reshape(1, 32),
+        dt_bias.reshape(1, 2),
+        decay_rate.reshape(1, 2),
+        skip_gain.reshape(1, 2),
+        norm_gain.reshape(1, 128),
+        jnp.transpose(tail_x, (1, 0, 2)),
+        jnp.transpose(tail_bc, (1, 0, 2)),
+    )
+    made = pl.pallas_call(
         kernel,
-        out_shape=(
-            jax.ShapeDtypeStruct((2, 2, 512), BF16),
-            jax.ShapeDtypeStruct((16, 128, 128), F32),
-            jax.ShapeDtypeStruct((16, 3, 128), BF16),
-            jax.ShapeDtypeStruct((16, 3, 32), BF16),
-        ),
-        in_specs=[hbm] * 6 + [vmem] * 4 + [smem] * 3 + [vmem] * 3,
-        out_specs=(vmem, hbm, vmem, vmem),
+        out_shape=tuple(V(v.shape, v.dtype) for v in shapes),
+        in_specs=[hbm] * 16,
+        out_specs=(vmem,) * 4,
         scratch_shapes=[
             V((2, 128, 512), BF16),
             V((1024, 128), BF16),
-            V((512, 32), BF16),
-            V((512, 2), BF16),
+            V((32, 512), BF16),
+            V((2, 512), BF16),
             V((16, 128, 128), F32),
+            V((4, 128), F32),
+            V((1, 128), F32),
+            V((4, 32), F32),
+            V((1, 32), F32),
+            V((1, 2), F32),
+            V((1, 2), F32),
+            V((1, 2), F32),
+            V((1, 128), F32),
+            V((3, 16, 128), BF16),
+            V((3, 16, 32), BF16),
             V((1024, 128), F32),
-            V((512, 256), BF16),
+            V((256, 512), BF16),
             V((512, 256), BF16),
             V((8, 32, 128), BF16),
             V((8, 32, 128), BF16),
@@ -372,46 +428,36 @@
             V((8, 16, 128), BF16),
             V((8, 16, 128), BF16),
             V((2, 1024, 256), BF16),
-            V((16, 8, 128), F32),
-            V((16, 8, 128), F32),
             V((32, 128), F32),
             V((32, 128), F32),
             V((256, 128), F32),
             V((32, 1024), BF16),
             V((8, 16, 128), F32),
             V((16, 128), F32),
-            V((16, 128, 128), F32),
-            dma((5,)),
+            dma((15,)),
             dma((6, 8)),
             dma((6, 8)),
             dma((8,)),
             dma((8,)),
             dma,
             dma,
-            dma,
+            pltpu.SemaphoreType.REGULAR,
+            pltpu.SemaphoreType.REGULAR,
         ],
         compiler_params=pltpu.CompilerParams(
-            collective_id=0, has_side_effects=True, vmem_limit_bytes=40 << 20
+            collective_id=0, has_side_effects=True, vmem_limit_bytes=32 << 20
         ),
-    )(
-        tokens,
-        w_zx.reshape(1024, 128),
-        w_bc,
-        w_dt,
-        w_out,
-        ssm_state.reshape(16, 128, 128),
-        conv_wx,
-        conv_bx.reshape(1, 128),
-        conv_wbc,
-        conv_bbc.reshape(1, 32),
-        dt_bias,
-        decay_rate,
-        skip_gain,
-        norm_gain.reshape(1, 128),
-        tail_x,
-        tail_bc,
-    )
-    return outs[0], outs[1].reshape(16, 2, 64, 128), outs[2], outs[3]
+    )(*(pltpu.with_memory_space_constraint(v, pltpu.HBM) for v in operands))
+    outs = pl.pallas_call(
+        hand_over,
+        out_shape=shapes,
+        in_specs=[pl.BlockSpec(memory_space=pl.ANY)] * 4,
+        out_specs=(hbm,) * 4,
+        scratch_shapes=[dma((4,))],
+        compiler_params=pltpu.CompilerParams(vmem_limit_bytes=32 << 20),
+    )(*made)
+    back = (1, 0, 2)
+    return outs[0], outs[1].reshape(16, 2, 64, 128), jnp.transpose(outs[2], back), jnp.transpose(outs[3], back)
 
 
 def solution(mesh):

time: 65.8 us -> 53 us (0.81)
  local copies, waits for them, and re-layouts: 8.38 us -> 0 us
  Pallas kernels: 56 us -> 51.8 us
    unnamed x34 -> x0, local copies, waits for them, and re-layouts: 8.38 us -> none
    pallas_call x1 -> x2, Pallas kernels: 56 us -> 51.8 us  [the longest x1 50.7 us: local(): pl.pallas_call(kernel, out_shape=tuple((V(v.shape, v.dtype) for v in shap...]
where the time goes in v2:
time: 53 us; the launch traced here: 52.4 us
  Pallas kernels  51.8 us (98%)
  between operations  0.65 us (1%)
    pallas_call x1, Pallas kernels, local(): pl.pallas_call(kernel, out_shape=tuple((V(v.shape, v.dtype) for v in shap...  50.7 us

profile of v2, /device:TPU:1, one launch (start us, length us, event | category | flops | bytes accessed | tf_op | source)
XLA Modules:
  0.0 52.4 jit_solution(3824648896446989024)
XLA Ops:
  0.6 50.7 %shard_map.183 = (bf16[2,2,512]{2,1,0:T(2,128)(2,1)S(1)}, f32[16,128,128]{2,1,0:T(8,128)S(1)}, bf16[3,16,128]{2,1,0:T(8,128)(2,1)S(1)}, bf16[3,16,32]{2,1,0:T(8,128)(2,1)S(1)}) custom-call(bf16[2,128,512]{2,1,0:T(8,128)(2,1)} %tokens_h.1, bf16[1024,128]{1,0:T(8,128)(2,1)} %bitcast.16, bf16[32,512]{1,0:T(8,128)(2,1)} %bitcast.17, bf16[2,512]{1,0:T(2,128)(2,1)} %bitcast.20, ...), custom_call_target="tpu_custom_call" | custom-call | tf_op jit(solution)/shard_map/pallas_call | solution.py:395
  51.4 1.0 %shard_map.184 = (bf16[2,2,512]{2,1,0:T(2,128)(2,1)}, f32[16,128,128]{2,1,0:T(8,128)}, bf16[3,16,128]{2,1,0:T(8,128)(2,1)}, bf16[3,16,32]{2,1,0:T(8,128)(2,1)}) custom-call(bf16[2,2,512]{2,1,0:T(2,128)(2,1)S(1)} %get-tuple-element.12.a, f32[16,128,128]{2,1,0:T(8,128)S(1)} %get-tuple-element.13.b, bf16[3,16,128]{2,1,0:T(8,128)(2,1)S(1)} %get-tuple-element.14.c, ...), custom_call_target="tpu_custom_call" | custom-call | tf_op jit(solution)/shard_map/pallas_call | solution.py:451

commit v3 on v2

--- a/solution.py
+++ b/solution.py
@@ -27,14 +27,15 @@
     tok, wz, wbc, wdt, st, conv_wx, conv_bx, conv_wbc, conv_bbc, dt_bias, decay_rate, skip_gain, norm_gain, tail_x, tail_bc,
     zf, wa, wgx,
     sa, ra, sb, rb, sc, rc, s3, r3, r4, s5, r5, wo,
-    gs, n4, f4, lhs, f5, o5,
-    lsem, ssem, rsem, wsend, wrecv, csend, crecv, near, far,
+    gs, f4, lhs, f5, o5,
+    lsem, ssem, rsem, wsend, wrecv, csend, crecv, near, far, xsend, xrecv,
 ):
     row = lax.axis_index("row")
     head = lax.axis_index("head")
     grp = lax.div(head, 8)
     mem = lax.rem(head, 8)
-    quart = lax.rem(head, 4)
+    quad = lax.div(head, 4)
+    place = lax.rem(head, 4)
     core = lax.rem(head, 2)
     owner_kind = lax.div(head, 32)
     bc_group = lax.div(lax.rem(head, 32), 4)
@@ -47,15 +48,16 @@
     chip = head - core
     for d in range(1, 8):
         signal(barrier, chip, lax.rem(row + d, 8))
-    for d in range(1, 4):
-        signal(barrier, grp * 8 + lax.rem(mem - core + 2 * d, 8), row)
+    other = quad * 4 + lax.rem(place - core + 2, 4)
+    signal(barrier, other, row)
 
     @pl.when(core == 1)
     def _():
         signal(barrier, chip, row)
 
-    for d in range(1, 8):
-        signal(barrier, lax.rem(chip + 8 * d, 64) + 1, row)
+    for d in range(1, 16):
+        signal(barrier, lax.rem(chip + 4 * d, 64) + 1, row)
+    signal(barrier, grp * 8 + lax.rem(mem - core + 4 + 2 - 4 * lax.div(lax.rem(mem, 4), 2), 8) + 1, row)
     for n in range(4):
         src = (n // 2) * 32 + grp * 4 + (n % 2) * 2
 
@@ -76,22 +78,21 @@
         load.start()
 
     loads[1].wait()
-    for n in range(4):
-        wa[n * 32 : n * 32 + 32, :] = wbc[...]
     loads[2].wait()
-    wd = wdt[...].astype(F32)
-    wa[128:, :] = jnp.where(iota((128, 512), 0) < 64, wd[0:1], wd[1:2]).astype(BF16)
+    steps = jnp.concatenate([wdt[...].astype(F32), jnp.zeros((30, 512), F32)], axis=0).astype(BF16)
+    for n in range(2):
+        wa[n * 64 : n * 64 + 32, :] = wbc[...]
+        wa[n * 64 + 32 : n * 64 + 64, :] = steps
     loads[0].wait()
     toks = tok[...].reshape(256, 512)
     pa = lax.dot_general(toks, wa[...], NT, preferred_element_type=F32)
+    pa = jnp.where(iota((128, 128), 1) < 64, pa[:128], pa[128:]).astype(BF16)
     for i in range(8):
-        for s in range(2):
-            sa[i, s * 16 : s * 16 + 16, :] = pa[s * 128 + i * 16 : s * 128 + i * 16 + 16, :128].astype(BF16)
-            sb[i, 2, s * 16 : s * 16 + 16, :] = pa[s * 128 + i * 16 : s * 128 + i * 16 + 16, 128:].astype(BF16)
+        sa[i] = pa[i * 16 : i * 16 + 16]
 
     @pl.when(core == 0)
     def _():
-        pl.semaphore_wait(barrier, 21)
+        pl.semaphore_wait(barrier, 17)
         signal(near, head + 1, row)
 
     @pl.when(core == 1)
@@ -125,17 +126,17 @@
         to = lax.rem(row + d, 8)
         sends.append(send(sb.at[to], rb.at[row], ssem.at[1, d], rsem.at[1, row], (head, to)))
 
-    for n in range(8):
+    for n in range(4):
         part = w_out.at[:, (n % 2) * 256 : (n % 2) * 256 + 256]
-        place = wo.at[n % 2, pl.ds(mem * 128, 128), :]
-
-        @pl.when(mem != n)
-        def _():
-            send(part, place, wsend.at[n], wrecv.at[mem], (grp * 8 + n, row))
-
-        @pl.when(mem == n)
-        def _():
-            pltpu.make_async_copy(part, place, wrecv.at[mem]).start()
+        spot = wo.at[n % 2, pl.ds(place * 128, 128), :]
+
+        @pl.when(place != n)
+        def _():
+            send(part, spot, wsend.at[n], wrecv.at[place], (quad * 4 + n, row))
+
+        @pl.when(place == n)
+        def _():
+            pltpu.make_async_copy(part, spot, wrecv.at[place]).start()
 
     ra[row] = sa[row]
     rb[row] = sb[row]
@@ -143,20 +144,11 @@
     for n in range(5, 15):
         loads[n].wait()
 
-    def windows(t, raw, weight, bias):
-        t0, t1, t2 = t
-        r0, r1 = raw[:16], raw[16:]
-        w = [weight[k : k + 1, :] for k in range(4)]
-        c0 = t0 * w[0] + t1 * w[1] + t2 * w[2] + r0 * w[3] + bias
-        c1 = t1 * w[0] + t2 * w[1] + r0 * w[2] + r1 * w[3] + bias
-        both = jnp.concatenate([c0, c1], axis=0)
-        return jax.nn.silu(both).astype(BF16)
-
-    def new_tail(ref, old, raw):
-        width = ref.shape[2]
-        ref[0] = old[2]
-        ref[1] = raw[:16, :width].astype(BF16)
-        ref[2] = raw[16:, :width].astype(BF16)
+    def taps(window, weight, bias):
+        summed = bias
+        for k in range(4):
+            summed = summed + window[k] * weight[k : k + 1, :]
+        return jax.nn.silu(summed).astype(BF16).astype(F32)
 
     old_bc = [jnp.concatenate([tail_bc[k].astype(F32)] * 4, axis=1) for k in range(3)]
     old_x = [tail_x[k].astype(F32) for k in range(3)]
@@ -172,20 +164,29 @@
     total = ra[0].astype(F32)
     for i in range(1, 8):
         total += ra[i].astype(F32)
-    raw_bc = total.astype(BF16).astype(F32)
-    conv_bc = windows(old_bc, raw_bc, weight_bc, bias_bc).astype(F32)
-    sc[...] = jnp.where(lax.div(iota((32, 128), 1), 32) == quart, conv_bc, 0.0).astype(BF16)
+    raw = total.astype(BF16).astype(F32)
+    lane = iota((16, 128), 1)
+    low = lane < 64
+    raw_bc = jnp.where(lane % 64 < 32, raw, pltpu.roll(raw, 32, 1))
+    window = (
+        jnp.where(low, old_bc[0], old_bc[1]),
+        jnp.where(low, old_bc[1], old_bc[2]),
+        jnp.where(low, old_bc[2], pltpu.roll(raw_bc, 64, 1)),
+        raw_bc,
+    )
+    conv_bc = taps(window, weight_bc, bias_bc)
+    sc[...] = jnp.where(lax.rem(lax.div(lane, 32), 2) == lax.rem(place, 2), conv_bc, 0.0).astype(BF16)
 
     @pl.when(core == 1)
     def _():
-        pl.semaphore_wait(barrier, jnp.where(grp == bc_group, 20, 22))
+        pl.semaphore_wait(barrier, jnp.where(grp == bc_group, 38, 40))
         signal(far, head - 1, row)
 
     @pl.when(core == 0)
     def _():
         pl.semaphore_wait(far, 1)
 
-    slot = owner_kind * 4 + quart
+    slot = owner_kind * 4 + place
     for n in range(8):
         to = bc_group * 8 + n
 
@@ -197,25 +198,35 @@
         def _():
             pltpu.make_async_copy(sc, rc.at[slot], rsem.at[2, slot]).start()
 
-    new_tail(tail_bc_out, tail_bc, raw_bc)
+    tail_bc_out[0] = tail_bc[2]
+    tail_bc_out[1] = raw[:, :32].astype(BF16)
+    tail_bc_out[2] = pltpu.roll(raw, 64, 1)[:, :32].astype(BF16)
 
     for d in range(1, 8):
         frm = lax.rem(row + d, 8)
         arrived(rb.at[frm], rsem.at[1, frm])
     mixed = []
-    for part in range(3):
+    for part in range(2):
         total = rb[0, part].astype(F32)
         for i in range(1, 8):
             total += rb[i, part].astype(F32)
         mixed.append(total.astype(BF16).astype(F32))
-    gate_raw, raw_x, dt_raw = mixed
-    xc = windows(old_x, raw_x, conv_wx[...], conv_bx[...]).astype(F32)
-    new_tail(tail_x_out, tail_x, raw_x)
+    gate_raw, raw_x = mixed
+    x0, x1 = raw_x[:16], raw_x[16:]
+    xc0 = taps((old_x[0], old_x[1], old_x[2], x0), conv_wx[...], conv_bx[...])
+    xc1 = taps((old_x[1], old_x[2], x0, x1), conv_wx[...], conv_bx[...])
+    xc = jnp.concatenate([xc0, xc1], axis=0)
+    tail_x_out[0] = tail_x[2]
+    tail_x_out[1] = x0.astype(BF16)
+    tail_x_out[2] = x1.astype(BF16)
     first = iota((1, 128), 1) < 64
 
     def per_head(ref):
         return jnp.where(first, ref[:, 0:1], ref[:, 1:2])
 
+    dt_raw = jnp.concatenate(
+        [jnp.where(first, raw[:, k : k + 1], raw[:, k + 1 : k + 2]) for k in (32, 96)], axis=0
+    )
     step_size = jax.nn.softplus(dt_raw + per_head(dt_bias))
     decay = jnp.exp(-step_size * per_head(decay_rate))
     a = step_size * xc
@@ -228,11 +239,14 @@
 
     for n in range(8):
         arrived(rc.at[n], rsem.at[2, n])
-    b = rc[0].astype(F32) + rc[1].astype(F32) + rc[2].astype(F32) + rc[3].astype(F32)
-    c = rc[4].astype(F32) + rc[5].astype(F32) + rc[6].astype(F32) + rc[7].astype(F32)
-    c_low = c.astype(BF16)
-    b0, b1 = b[:16], b[16:]
-    c0, c1 = c[:16], c[16:]
+    def channels(k):
+        u = rc[k].astype(F32) + rc[k + 1].astype(F32)
+        v = rc[k + 2].astype(F32) + rc[k + 3].astype(F32)
+        return jnp.where(low, u, pltpu.roll(v, 64, 1)), jnp.where(low, pltpu.roll(u, 64, 1), v)
+
+    b0, b1 = channels(0)
+    c0, c1 = channels(4)
+    c_low = jnp.concatenate([c0, c1], axis=0).astype(BF16)
     mod16 = iota((32, 128), 0) % 16
     read = jnp.zeros((32, 128), F32)
     for r in range(16):
@@ -248,15 +262,15 @@
     gs[...] = gated
     s3[...] = jnp.zeros_like(s3)
     s3r = s3.reshape(64, 128)
-    for s in range(2):
-        for k in range(2):
-            s3r[pl.ds(s * 2 + k, 8, stride=8), :] = gs[pl.ds(s * 16 + k, 8, stride=2), :]
-    s3r[pl.ds(4, 8, stride=8), :] = jnp.broadcast_to(norm_gain[...], (8, 128))
+    for k in range(8):
+        p, t, u = k // 4, k // 2 % 2, k % 2
+        s3r[pl.ds(k, 4, stride=16), :] = gs[pl.ds(t * 16 + p * 8 + u, 4, stride=2), :]
+    s3r[pl.ds(8, 4, stride=16), :] = jnp.broadcast_to(norm_gain[...], (4, 128))
 
     for d in range(1, 8):
         to = lax.rem(mem + d, 8)
-        sends.append(send(s3.at[to], r3.at[mem], ssem.at[3, d], rsem.at[3, mem], (grp * 8 + to, row)))
-    r3[mem] = s3[mem]
+        sends.append(send(s3.at[lax.rem(to, 4)], r3.at[mem], ssem.at[3, d], rsem.at[3, mem], (grp * 8 + to, row)))
+    r3[mem] = s3[place]
 
     def high_low(v):
         high = v.astype(BF16).astype(F32)
@@ -287,17 +301,15 @@
         arrived(r3.at[frm], rsem.at[3, frm])
     square = jnp.zeros((8, 128), F32)
     for n in range(8):
-        square += r3[n] * r3[n]
+        square += r3[n, 0:8, :] * r3[n, 0:8, :]
     scale = lax.rsqrt(jnp.sum(square, axis=1, keepdims=True) / 1024.0 + EPS)
-    for n in range(8):
-        block = r3[n]
-        n4[n * 4 : n * 4 + 4, :] = (block * scale * block[4:5, :])[:4]
-    r4[row] = n4[...].astype(BF16)
+    blocks = [r3[lax.div(mem, 4) * 4 + n] for n in range(4)]
+    r4[row] = jnp.concatenate([v[0:8] * scale * v[8:9] for v in blocks], axis=0).astype(BF16)
     for d in range(1, 8):
         to = lax.rem(row + d, 8)
         sends.append(send(r4.at[row], r4.at[row], ssem.at[4, d], rsem.at[4, row], (head, to)))
 
-    for n in range(8):
+    for n in range(4):
         arrived(wo.at[core, pl.ds(n * 128, 128), :], wrecv.at[n])
     sibling = head + 1 - 2 * core
     sends.append(send(wo.at[core], wo.at[core], csend, crecv, (sibling, row)))
@@ -309,26 +321,27 @@
         frm = lax.rem(row + d, 8)
         arrived(r4.at[frm], rsem.at[4, frm])
     f4[...] = r4[...].reshape(256, 128).astype(F32)
-    for n in range(8):
-        block = [f4[pl.ds(n * 4 + rr, 8, stride=32), :] for rr in range(4)]
+    for n in range(4):
+        block = [f4[pl.ds(n * 8 + k, 8, stride=32), :] for k in range(8)]
         lhs[:, n * 128 : n * 128 + 128] = jnp.concatenate(block, axis=0).astype(BF16)
     arrived(wo.at[1 - core], crecv)
-    f5r = f5.reshape(128, 128)
+    f5r = f5.reshape(256, 128)
     for half in range(2):
         out = dot(lhs[...], wo[half])
-        for rr in range(4):
+        for n in range(8):
             for k in range(2):
-                f5r[pl.ds(rr * 4 + half * 2 + k, 8, stride=16), :] = out[rr * 8 : rr * 8 + 8, k * 128 : k * 128 + 128]
+                at = n // 4 * 16 + n % 4 * 4 + half * 2 + k
+                f5r[pl.ds(at, 8, stride=32), :] = out[n * 8 : n * 8 + 8, k * 128 : k * 128 + 128]
     s5[...] = f5[...].astype(BF16)
-    for d in range(1, 8):
-        to = lax.rem(grp + d, 8)
-        sends.append(send(s5.at[to], r5.at[grp], ssem.at[5, d], rsem.at[5, grp], (to * 8 + mem, row)))
-    r5[grp] = s5[grp]
-    for d in range(1, 8):
-        frm = lax.rem(grp + d, 8)
-        arrived(r5.at[frm], rsem.at[5, frm])
+    for d in range(1, 16):
+        to = lax.rem(quad + d, 16)
+        sends.append(send(s5.at[to], r5.at[quad], xsend.at[d], xrecv.at[quad], (to * 4 + place, row)))
+    r5[quad] = s5[quad]
+    for d in range(1, 16):
+        frm = lax.rem(quad + d, 16)
+        arrived(r5.at[frm], xrecv.at[frm])
     total = r5[0].astype(F32)
-    for i in range(1, 8):
+    for i in range(1, 16):
         total += r5[i].astype(F32)
     o5[...] = total
     for s in range(2):
@@ -338,11 +351,13 @@
 
     for copy in sends:
         copy.wait_send()
+    for n in range(4):
+
+        @pl.when(place != n)
+        def _():
+            arrived(w_out.at[:, 0:256], wsend.at[n])
+
     for n in range(8):
-
-        @pl.when(mem != n)
-        def _():
-            arrived(w_out.at[:, 0:256], wsend.at[n])
 
         @pl.when(bc_group * 8 + n != head)
         def _():
@@ -414,35 +429,36 @@
             V((3, 16, 128), BF16),
             V((3, 16, 32), BF16),
             V((1024, 128), F32),
-            V((256, 512), BF16),
+            V((128, 512), BF16),
             V((512, 256), BF16),
-            V((8, 32, 128), BF16),
-            V((8, 32, 128), BF16),
-            V((8, 3, 32, 128), BF16),
-            V((8, 3, 32, 128), BF16),
-            V((32, 128), BF16),
-            V((8, 32, 128), BF16),
-            V((8, 8, 128), F32),
-            V((8, 8, 128), F32),
-            V((8, 32, 128), BF16),
             V((8, 16, 128), BF16),
             V((8, 16, 128), BF16),
-            V((2, 1024, 256), BF16),
-            V((32, 128), F32),
+            V((8, 2, 32, 128), BF16),
+            V((8, 2, 32, 128), BF16),
+            V((16, 128), BF16),
+            V((8, 16, 128), BF16),
+            V((4, 16, 128), F32),
+            V((8, 16, 128), F32),
+            V((8, 32, 128), BF16),
+            V((16, 16, 128), BF16),
+            V((16, 16, 128), BF16),
+            V((2, 512, 256), BF16),
             V((32, 128), F32),
             V((256, 128), F32),
-            V((32, 1024), BF16),
-            V((8, 16, 128), F32),
+            V((64, 512), BF16),
+            V((16, 16, 128), F32),
             V((16, 128), F32),
             dma((15,)),
-            dma((6, 8)),
-            dma((6, 8)),
-            dma((8,)),
-            dma((8,)),
+            dma((5, 8)),
+            dma((5, 8)),
+            dma((4,)),
+            dma((4,)),
             dma,
             dma,
             pltpu.SemaphoreType.REGULAR,
             pltpu.SemaphoreType.REGULAR,
+            dma((16,)),
+            dma((16,)),
         ],
         compiler_params=pltpu.CompilerParams(
             collective_id=0, has_side_effects=True, vmem_limit_bytes=32 << 20

time: 53 us -> 43.7 us (0.82)
  Pallas kernels: 51.8 us -> 42.7 us
    pallas_call x1, Pallas kernels: 50.7 us -> 41.6 us  [local(): pl.pallas_call(kernel, out_shape=tuple((V(v.shape, v.dtype) for v in shap...]
where the time goes in v3:
time: 43.7 us; the launch traced here: 43.3 us
  Pallas kernels  42.7 us (98%)
  between operations  0.65 us (1%)
    pallas_call x1, Pallas kernels, local(): pl.pallas_call(kernel, out_shape=tuple((V(v.shape, v.dtype) for v in shap...  41.6 us
    pallas_call x1, Pallas kernels, local(): pl.pallas_call(hand_over, out_shape=shapes, in_specs=[pl.BlockSpec(memory...  1.02 us

profile of v3, /device:TPU:1, one launch (start us, length us, event | category | flops | bytes accessed | tf_op | source)
XLA Modules:
  0.0 43.3 jit_solution(3487085823592676400)
XLA Ops:
  0.6 41.6 %shard_map.183 = (bf16[2,2,512]{2,1,0:T(2,128)(2,1)S(1)}, f32[16,128,128]{2,1,0:T(8,128)S(1)}, bf16[3,16,128]{2,1,0:T(8,128)(2,1)S(1)}, bf16[3,16,32]{2,1,0:T(8,128)(2,1)S(1)}) custom-call(bf16[2,128,512]{2,1,0:T(8,128)(2,1)} %tokens_h.1, bf16[1024,128]{1,0:T(8,128)(2,1)} %bitcast.16, bf16[32,512]{1,0:T(8,128)(2,1)} %bitcast.17, bf16[2,512]{1,0:T(2,128)(2,1)} %bitcast.20, ...), custom_call_target="tpu_custom_call" | custom-call | tf_op jit(solution)/shard_map/pallas_call | solution.py:410
  42.3 1.0 %shard_map.184 = (bf16[2,2,512]{2,1,0:T(2,128)(2,1)}, f32[16,128,128]{2,1,0:T(8,128)}, bf16[3,16,128]{2,1,0:T(8,128)(2,1)}, bf16[3,16,32]{2,1,0:T(8,128)(2,1)}) custom-call(bf16[2,2,512]{2,1,0:T(2,128)(2,1)S(1)} %get-tuple-element.12.a, f32[16,128,128]{2,1,0:T(8,128)S(1)} %get-tuple-element.13.b, bf16[3,16,128]{2,1,0:T(8,128)(2,1)S(1)} %get-tuple-element.14.c, ...), custom_call_target="tpu_custom_call" | custom-call | tf_op jit(solution)/shard_map/pallas_call | solution.py:467

commit v4 on v3

--- a/solution.py
+++ b/solution.py
@@ -23,12 +23,12 @@
 def kernel(
     tokens_h, w_zx_h, w_bc_h, w_dt_h, w_out, state_h,
     conv_wx_h, conv_bx_h, conv_wbc_h, conv_bbc_h, dt_bias_h, decay_rate_h, skip_gain_h, norm_gain_h, tail_x_h, tail_bc_h,
-    layer_out, so, tail_x_out, tail_bc_out,
+    parts, squares, so, tail_x_out, tail_bc_out,
     tok, wz, wbc, wdt, st, conv_wx, conv_bx, conv_wbc, conv_bbc, dt_bias, decay_rate, skip_gain, norm_gain, tail_x, tail_bc,
     zf, wa, wgx,
-    sa, ra, sb, rb, sc, rc, s3, r3, r4, s5, r5, wo,
-    gs, f4, lhs, f5, o5,
-    lsem, ssem, rsem, wsend, wrecv, csend, crecv, near, far, xsend, xrecv,
+    sa, ra, sb, rb, sc, rc, s3, s3b, r3, r4, s5, r5, sq, rq, wo,
+    gs, f4, lhs, f5, sl,
+    lsem, ssem, rsem, wsend, wrecv, csend, crecv, near, far, xsend, xrecv, qsend, qrecv,
 ):
     row = lax.axis_index("row")
     head = lax.axis_index("head")
@@ -40,14 +40,31 @@
     owner_kind = lax.div(head, 32)
     bc_group = lax.div(lax.rem(head, 32), 4)
 
+    sources = (
+        tokens_h, w_bc_h, w_dt_h, w_zx_h, state_h, conv_wbc_h, conv_bbc_h, tail_bc_h,
+        conv_wx_h, conv_bx_h, dt_bias_h, decay_rate_h, skip_gain_h, norm_gain_h, tail_x_h,
+    )
+    targets = (
+        tok, wbc, wdt, wz, st, conv_wbc, conv_bbc, tail_bc,
+        conv_wx, conv_bx, dt_bias, decay_rate, skip_gain, norm_gain, tail_x,
+    )
+    loads = [pltpu.make_async_copy(a, b, lsem.at[n]) for n, (a, b) in enumerate(zip(sources, targets))]
+    for load in loads[:3]:
+        load.start()
+
     barrier = pltpu.get_barrier_semaphore()
 
     def signal(sem, h, r):
         pl.semaphore_signal(sem, inc=1, device_id=(h, r), device_id_type=MESH)
 
+    def row_peer(dy, dx):
+        return lax.rem(row - x_hi + 2 * dy, 8) + lax.rem(x_hi + dx, 2)
+
+    x_hi = lax.rem(row, 2)
+    row_peers = [row_peer(dy, dx) for dy, dx in ((2, 1), (1, 1), (3, 1), (2, 0), (0, 1), (1, 0), (3, 0))]
     chip = head - core
-    for d in range(1, 8):
-        signal(barrier, chip, lax.rem(row + d, 8))
+    for peer in row_peers:
+        signal(barrier, chip, peer)
     other = quad * 4 + lax.rem(place - core + 2, 4)
     signal(barrier, other, row)
 
@@ -55,27 +72,16 @@
     def _():
         signal(barrier, chip, row)
 
+    for load in loads[3:]:
+        load.start()
     for d in range(1, 16):
         signal(barrier, lax.rem(chip + 4 * d, 64) + 1, row)
-    signal(barrier, grp * 8 + lax.rem(mem - core + 4 + 2 - 4 * lax.div(lax.rem(mem, 4), 2), 8) + 1, row)
     for n in range(4):
         src = (n // 2) * 32 + grp * 4 + (n % 2) * 2
 
         @pl.when(src != chip)
         def _():
             signal(barrier, src + 1, row)
-
-    sources = (
-        tokens_h, w_bc_h, w_dt_h, w_zx_h, state_h, conv_wbc_h, conv_bbc_h, tail_bc_h,
-        conv_wx_h, conv_bx_h, dt_bias_h, decay_rate_h, skip_gain_h, norm_gain_h, tail_x_h,
-    )
-    targets = (
-        tok, wbc, wdt, wz, st, conv_wbc, conv_bbc, tail_bc,
-        conv_wx, conv_bx, dt_bias, decay_rate, skip_gain, norm_gain, tail_x,
-    )
-    loads = [pltpu.make_async_copy(a, b, lsem.at[n]) for n, (a, b) in enumerate(zip(sources, targets))]
-    for load in loads:
-        load.start()
 
     loads[1].wait()
     loads[2].wait()
@@ -100,7 +106,6 @@
         pl.semaphore_wait(near, 1)
 
 
-    sends = []
     def send(src, dst, ss, rs, device):
         copy = pltpu.make_async_remote_copy(
             src_ref=src, dst_ref=dst, send_sem=ss, recv_sem=rs, device_id=device, device_id_type=MESH
@@ -108,9 +113,8 @@
         copy.start()
         return copy
 
-    for d in range(1, 8):
-        to = lax.rem(row + d, 8)
-        sends.append(send(sa.at[to], ra.at[row], ssem.at[0, d], rsem.at[0, row], (head, to)))
+    for to in row_peers:
+        send(sa.at[to], ra.at[row], ssem.at[0], rsem.at[0], (head, to))
 
     loads[3].wait()
     zf[...] = wz[...].astype(F32)
@@ -122,9 +126,8 @@
             piece = pz[s * 128 + i * 16 : s * 128 + i * 16 + 16, :].astype(BF16)
             sb[i, 0, s * 16 : s * 16 + 16, :] = piece[:, :128]
             sb[i, 1, s * 16 : s * 16 + 16, :] = piece[:, 128:]
-    for d in range(1, 8):
-        to = lax.rem(row + d, 8)
-        sends.append(send(sb.at[to], rb.at[row], ssem.at[1, d], rsem.at[1, row], (head, to)))
+    for to in row_peers:
+        send(sb.at[to], rb.at[row], ssem.at[1], rsem.at[1], (head, to))
 
     for n in range(4):
         part = w_out.at[:, (n % 2) * 256 : (n % 2) * 256 + 256]
@@ -132,11 +135,11 @@
 
         @pl.when(place != n)
         def _():
-            send(part, spot, wsend.at[n], wrecv.at[place], (quad * 4 + n, row))
+            send(part, spot, wsend, wrecv, (quad * 4 + n, row))
 
         @pl.when(place == n)
         def _():
-            pltpu.make_async_copy(part, spot, wrecv.at[place]).start()
+            pltpu.make_async_copy(part, spot, wrecv).start()
 
     ra[row] = sa[row]
     rb[row] = sb[row]
@@ -158,9 +161,7 @@
     def arrived(buf, sem):
         pltpu.make_async_copy(buf, buf, sem).wait()
 
-    for d in range(1, 8):
-        frm = lax.rem(row + d, 8)
-        arrived(ra.at[frm], rsem.at[0, frm])
+    arrived(ra.at[0:7], rsem.at[0])
     total = ra[0].astype(F32)
     for i in range(1, 8):
         total += ra[i].astype(F32)
@@ -179,7 +180,7 @@
 
     @pl.when(core == 1)
     def _():
-        pl.semaphore_wait(barrier, jnp.where(grp == bc_group, 38, 40))
+        pl.semaphore_wait(barrier, jnp.where(grp == bc_group, 36, 38))
         signal(far, head - 1, row)
 
     @pl.when(core == 0)
@@ -192,19 +193,17 @@
 
         @pl.when(to != head)
         def _():
-            send(sc, rc.at[slot], ssem.at[2, n], rsem.at[2, slot], (to, row))
+            send(sc, rc.at[slot], ssem.at[2], rsem.at[2], (to, row))
 
         @pl.when(to == head)
         def _():
-            pltpu.make_async_copy(sc, rc.at[slot], rsem.at[2, slot]).start()
+            pltpu.make_async_copy(sc, rc.at[slot], rsem.at[2]).start()
 
     tail_bc_out[0] = tail_bc[2]
     tail_bc_out[1] = raw[:, :32].astype(BF16)
     tail_bc_out[2] = pltpu.roll(raw, 64, 1)[:, :32].astype(BF16)
 
-    for d in range(1, 8):
-        frm = lax.rem(row + d, 8)
-        arrived(rb.at[frm], rsem.at[1, frm])
+    arrived(rb.at[0:7], rsem.at[1])
     mixed = []
     for part in range(2):
         total = rb[0, part].astype(F32)
@@ -236,9 +235,13 @@
     d01 = d0 * d1
     a0, a1 = a[:16], a[16:]
     loads[4].wait()
-
-    for n in range(8):
-        arrived(rc.at[n], rsem.at[2, n])
+    for r in range(16):
+        sl[:, r * 128 : r * 128 + 128] = st[r].astype(BF16)
+
+    arrived(ra.at[0:7], ssem.at[0])
+    arrived(rb.at[0:7], ssem.at[1])
+    arrived(wo.at[0, 0:384, :], wsend)
+    arrived(rc, rsem.at[2])
     def channels(k):
         u = rc[k].astype(F32) + rc[k + 1].astype(F32)
         v = rc[k + 2].astype(F32) + rc[k + 3].astype(F32)
@@ -248,10 +251,9 @@
     c0, c1 = channels(4)
     c_low = jnp.concatenate([c0, c1], axis=0).astype(BF16)
     mod16 = iota((32, 128), 0) % 16
-    read = jnp.zeros((32, 128), F32)
-    for r in range(16):
-        one = lax.dot_general(c_low, st[r].astype(BF16), NT, preferred_element_type=F32)
-        read = jnp.where(mod16 == r, one, read)
+    zero_low = jnp.zeros((32, 128), BF16)
+    spread = jnp.concatenate([jnp.where(mod16 == r, c_low, zero_low) for r in range(16)], axis=1)
+    read = lax.dot_general(spread, sl[...], NT, preferred_element_type=F32)
 
     def along(u, v):
         return jnp.sum(u * v, axis=1, keepdims=True)
@@ -265,12 +267,15 @@
     for k in range(8):
         p, t, u = k // 4, k // 2 % 2, k % 2
         s3r[pl.ds(k, 4, stride=16), :] = gs[pl.ds(t * 16 + p * 8 + u, 4, stride=2), :]
-    s3r[pl.ds(8, 4, stride=16), :] = jnp.broadcast_to(norm_gain[...], (4, 128))
-
-    for d in range(1, 8):
-        to = lax.rem(mem + d, 8)
-        sends.append(send(s3.at[lax.rem(to, 4)], r3.at[mem], ssem.at[3, d], rsem.at[3, mem], (grp * 8 + to, row)))
-    r3[mem] = s3[place]
+    gain_high = norm_gain[...].astype(BF16).astype(F32)
+    s3r[pl.ds(8, 4, stride=16), :] = jnp.broadcast_to(gain_high, (4, 128))
+    s3r[pl.ds(9, 4, stride=16), :] = jnp.broadcast_to(norm_gain[...] - gain_high, (4, 128))
+    s3b[...] = s3[...].astype(BF16)
+
+    for d in range(1, 4):
+        to = lax.rem(place + d, 4)
+        send(s3b.at[to], r3.at[place], ssem.at[3], rsem.at[3], (quad * 4 + to, row))
+    r3[place] = s3b[place]
 
     def high_low(v):
         high = v.astype(BF16).astype(F32)
@@ -296,33 +301,38 @@
     for r in range(8):
         update(r)
 
-    for d in range(1, 8):
-        frm = lax.rem(mem + d, 8)
-        arrived(r3.at[frm], rsem.at[3, frm])
-    square = jnp.zeros((8, 128), F32)
-    for n in range(8):
-        square += r3[n, 0:8, :] * r3[n, 0:8, :]
-    scale = lax.rsqrt(jnp.sum(square, axis=1, keepdims=True) / 1024.0 + EPS)
-    blocks = [r3[lax.div(mem, 4) * 4 + n] for n in range(4)]
-    r4[row] = jnp.concatenate([v[0:8] * scale * v[8:9] for v in blocks], axis=0).astype(BF16)
-    for d in range(1, 8):
-        to = lax.rem(row + d, 8)
-        sends.append(send(r4.at[row], r4.at[row], ssem.at[4, d], rsem.at[4, row], (head, to)))
-
-    for n in range(4):
-        arrived(wo.at[core, pl.ds(n * 128, 128), :], wrecv.at[n])
+    arrived(r3.at[0:3], rsem.at[3])
+    blocks = [r3[n].astype(F32) for n in range(4)]
+    square = sum(v[0:8] * v[0:8] for v in blocks)
+    square = jnp.broadcast_to(jnp.sum(square, axis=1, keepdims=True), (8, 128))
+    rows = [v[0:8] * (v[8:9] + v[9:10]) for v in blocks] + [square, jnp.zeros((8, 128), F32)]
+    r4[row] = jnp.concatenate(rows, axis=0).astype(BF16)
+    for to in row_peers:
+        send(r4.at[row], r4.at[row], ssem.at[4], rsem.at[4], (head, to))
+    arrived(r3.at[0:3], ssem.at[3])
+
+    arrived(wo.at[core], wrecv)
     sibling = head + 1 - 2 * core
-    sends.append(send(wo.at[core], wo.at[core], csend, crecv, (sibling, row)))
+    send(wo.at[core], wo.at[core], csend, crecv, (sibling, row))
 
     for r in range(8, 16):
         update(r)
 
-    for d in range(1, 8):
-        frm = lax.rem(row + d, 8)
-        arrived(r4.at[frm], rsem.at[4, frm])
-    f4[...] = r4[...].reshape(256, 128).astype(F32)
+    arrived(r4.at[0:7], rsem.at[4])
+    f4[...] = r4[...].reshape(384, 128).astype(F32)
+    which_row = lax.div(iota((8, 128), 1), 32)
+    for p in range(2):
+        square = f4[pl.ds(32 + p * 4, 8, stride=48), :]
+        for n in range(1, 4):
+            square = jnp.where(which_row == n, f4[pl.ds(32 + p * 4 + n, 8, stride=48), :], square)
+        for i in range(8):
+            sq[2 * i + p] = square[i : i + 1]
+    for d in (4, 12, 3, 5, 11, 13, 2, 6, 10, 14, 1, 7, 9, 15, 8):
+        to = lax.rem(quad + d, 16)
+        send(sq.at[to], rq.at[quad], qsend, qrecv, (to * 4 + place, row))
+    rq[quad] = sq[quad]
     for n in range(4):
-        block = [f4[pl.ds(n * 8 + k, 8, stride=32), :] for k in range(8)]
+        block = [f4[pl.ds(n * 8 + k, 8, stride=48), :] for k in range(8)]
         lhs[:, n * 128 : n * 128 + 128] = jnp.concatenate(block, axis=0).astype(BF16)
     arrived(wo.at[1 - core], crecv)
     f5r = f5.reshape(256, 128)
@@ -333,46 +343,50 @@
                 at = n // 4 * 16 + n % 4 * 4 + half * 2 + k
                 f5r[pl.ds(at, 8, stride=32), :] = out[n * 8 : n * 8 + 8, k * 128 : k * 128 + 128]
     s5[...] = f5[...].astype(BF16)
-    for d in range(1, 16):
+    for d in (4, 12, 3, 5, 11, 13, 2, 6, 10, 14, 1, 7, 9, 15, 8):
         to = lax.rem(quad + d, 16)
-        sends.append(send(s5.at[to], r5.at[quad], xsend.at[d], xrecv.at[quad], (to * 4 + place, row)))
+        send(s5.at[to], r5.at[quad], xsend, xrecv, (to * 4 + place, row))
     r5[quad] = s5[quad]
-    for d in range(1, 16):
-        frm = lax.rem(quad + d, 16)
-        arrived(r5.at[frm], xrecv.at[frm])
-    total = r5[0].astype(F32)
-    for i in range(1, 16):
-        total += r5[i].astype(F32)
+    arrived(r4.at[0:7], ssem.at[4])
+    arrived(wo.at[core], csend)
+
+    @pl.when(grp == bc_group)
+    def _():
+        arrived(rc.at[0:7], ssem.at[2])
+
+    @pl.when(grp != bc_group)
+    def _():
+        arrived(rc, ssem.at[2])
+
+    arrived(r5.at[0:15], xsend)
+    arrived(r5.at[0:15], xrecv)
+    arrived(rq.at[0:15], qsend)
+    arrived(rq.at[0:15], qrecv)
+    parts[...] = r5[...]
+    squares[...] = rq[...]
+
+
+def hand_over(parts, squares, a, b, c, layer_out, oa, ob, oc, made, o5, sem):
+    moves = [(a.at[4 * n : 4 * n + 4], oa.at[4 * n : 4 * n + 4]) for n in range(4)] + [(b, ob), (c, oc)]
+    copies = [pltpu.make_async_copy(src, dst, sem.at[n]) for n, (src, dst) in enumerate(moves)]
+    for copy in copies:
+        copy.start()
+    total = jnp.zeros((16, 128), F32)
+    mine = lax.div(iota((16, 128), 0), 4) * 32 == iota((16, 128), 1)
+    for i in range(8):
+        both = parts[2 * i].astype(F32) + parts[2 * i + 1].astype(F32)
+        scale = lax.rsqrt((squares[2 * i] + squares[2 * i + 1]) / 1024.0 + EPS)
+        total += both * jnp.sum(jnp.where(mine, scale, 0.0), axis=1, keepdims=True)
     o5[...] = total
     for s in range(2):
         for k in range(4):
             pair = o5[pl.ds(s * 8 + k, 2, stride=4), :]
-            layer_out[s, :, k * 128 : k * 128 + 128] = pair.astype(BF16)
-
-    for copy in sends:
-        copy.wait_send()
-    for n in range(4):
-
-        @pl.when(place != n)
-        def _():
-            arrived(w_out.at[:, 0:256], wsend.at[n])
-
-    for n in range(8):
-
-        @pl.when(bc_group * 8 + n != head)
-        def _():
-            arrived(sc, ssem.at[2, n])
-
-
-def hand_over(a, b, c, d, oa, ob, oc, od, sem):
-    copies = [
-        pltpu.make_async_copy(src, dst, sem.at[n])
-        for n, (src, dst) in enumerate(((a, oa), (b, ob), (c, oc), (d, od)))
-    ]
-    for copy in copies:
-        copy.start()
+            made[s, :, k * 128 : k * 128 + 128] = pair.astype(BF16)
+    last = pltpu.make_async_copy(made, layer_out, sem.at[6])
+    last.start()
     for copy in copies:
         copy.wait()
+    last.wait()
 
 
 def local(
@@ -409,9 +423,9 @@
     )
     made = pl.pallas_call(
         kernel,
-        out_shape=tuple(V(v.shape, v.dtype) for v in shapes),
+        out_shape=(V((16, 16, 128), BF16), V((16, 1, 128), F32), *(V(v.shape, v.dtype) for v in shapes[1:])),
         in_specs=[hbm] * 16,
-        out_specs=(vmem,) * 4,
+        out_specs=(vmem,) * 5,
         scratch_shapes=[
             V((2, 128, 512), BF16),
             V((1024, 128), BF16),
@@ -438,27 +452,32 @@
             V((16, 128), BF16),
             V((8, 16, 128), BF16),
             V((4, 16, 128), F32),
-            V((8, 16, 128), F32),
-            V((8, 32, 128), BF16),
+            V((4, 16, 128), BF16),
+            V((4, 16, 128), BF16),
+            V((8, 48, 128), BF16),
             V((16, 16, 128), BF16),
             V((16, 16, 128), BF16),
+            V((16, 1, 128), F32),
+            V((16, 1, 128), F32),
             V((2, 512, 256), BF16),
             V((32, 128), F32),
-            V((256, 128), F32),
+            V((384, 128), F32),
             V((64, 512), BF16),
             V((16, 16, 128), F32),
-            V((16, 128), F32),
+            V((128, 2048), BF16),
             dma((15,)),
-            dma((5, 8)),
-            dma((5, 8)),
-            dma((4,)),
-            dma((4,)),
+            dma((5,)),
+            dma((5,)),
+            dma,
+            dma,
             dma,
             dma,
             pltpu.SemaphoreType.REGULAR,
             pltpu.SemaphoreType.REGULAR,
-            dma((16,)),
-            dma((16,)),
+            dma,
+            dma,
+            dma,
+            dma,
         ],
         compiler_params=pltpu.CompilerParams(
             collective_id=0, has_side_effects=True, vmem_limit_bytes=32 << 20
@@ -467,9 +486,9 @@
     outs = pl.pallas_call(
         hand_over,
         out_shape=shapes,
-        in_specs=[pl.BlockSpec(memory_space=pl.ANY)] * 4,
+        in_specs=[vmem, vmem] + [pl.BlockSpec(memory_space=pl.ANY)] * 3,
         out_specs=(hbm,) * 4,
-        scratch_shapes=[dma((4,))],
+        scratch_shapes=[V((2, 2, 512), BF16), V((16, 128), F32), dma((7,))],
         compiler_params=pltpu.CompilerParams(vmem_limit_bytes=32 << 20),
     )(*made)
     back = (1, 0, 2)

time: 43.7 us -> 41.5 us (0.950)
  Pallas kernels: 42.7 us -> 40.7 us
    pallas_call x2, Pallas kernels: 42.7 us -> 40.7 us  [the longest x1 39.7 us: local(): pl.pallas_call(kernel, out_shape=(V((16, 16, 128), BF16), V((16, 1, 128),...]
where the time goes in v4:
time: 41.5 us; the launch traced here: 41.3 us
  Pallas kernels  40.7 us (98%)
  between operations  0.65 us (2%)
    pallas_call x1, Pallas kernels, local(): pl.pallas_call(kernel, out_shape=(V((16, 16, 128), BF16), V((16, 1, 128),...  39.7 us
    pallas_call x1, Pallas kernels, local(): pl.pallas_call(hand_over, out_shape=shapes, in_specs=[vmem, vmem] + [pl.B...  1.03 us

profile of v4, /device:TPU:1, one launch (start us, length us, event | category | flops | bytes accessed | tf_op | source)
XLA Modules:
  0.0 41.3 jit_solution(6612815841551732211)
XLA Ops:
  0.6 39.7 %shard_map.183 = (bf16[16,16,128]{2,1,0:T(8,128)(2,1)S(1)}, f32[16,1,128]{2,1,0:T(1,128)S(1)}, f32[16,128,128]{2,1,0:T(8,128)S(1)}, bf16[3,16,128]{2,1,0:T(8,128)(2,1)S(1)}, bf16[3,16,32]{2,1,0:T(8,128)(2,1)S(1)}) custom-call(bf16[2,128,512]{2,1,0:T(8,128)(2,1)} %tokens_h.1, bf16[1024,128]{1,0:T(8,128)(2,1)} %bitcast.16, bf16[32,512]{1,0:T(8,128)(2,1)} %bitcast.17, ...), custom_call_target="tpu_custom_call" | custom-call | tf_op jit(solution)/shard_map/pallas_call | solution.py:424
  40.3 1.0 %shard_map.184 = (bf16[2,2,512]{2,1,0:T(2,128)(2,1)}, f32[16,128,128]{2,1,0:T(8,128)}, bf16[3,16,128]{2,1,0:T(8,128)(2,1)}, bf16[3,16,32]{2,1,0:T(8,128)(2,1)}) custom-call(bf16[16,16,128]{2,1,0:T(8,128)(2,1)S(1)} %get-tuple-element.13.parts, f32[16,1,128]{2,1,0:T(1,128)S(1)} %get-tuple-element.14.squares, f32[16,128,128]{2,1,0:T(8,128)S(1)} %get-tuple-element.15.a, ...), custom_call_target="tpu_custom_call" | custom-call | tf_op jit(solution)/shard_map/pallas_call | solution.py:486

commit v5 on v4

--- a/solution.py
+++ b/solution.py
@@ -27,8 +27,8 @@
     tok, wz, wbc, wdt, st, conv_wx, conv_bx, conv_wbc, conv_bbc, dt_bias, decay_rate, skip_gain, norm_gain, tail_x, tail_bc,
     zf, wa, wgx,
     sa, ra, sb, rb, sc, rc, s3, s3b, r3, r4, s5, r5, sq, rq, wo,
-    gs, f4, lhs, f5, sl,
-    lsem, ssem, rsem, wsend, wrecv, csend, crecv, near, far, xsend, xrecv, qsend, qrecv,
+    gs, f5, sl,
+    lsem, ssem, rsem, wsend, wrecv, csend, crecv, near, far, xsend, xrecv, qsend, qrecv, rowsem,
 ):
     row = lax.axis_index("row")
     head = lax.axis_index("head")
@@ -277,6 +277,10 @@
         send(s3b.at[to], r3.at[place], ssem.at[3], rsem.at[3], (quad * 4 + to, row))
     r3[place] = s3b[place]
 
+    arrived(wo.at[core], wrecv)
+    sibling = head + 1 - 2 * core
+    send(wo.at[core], wo.at[core], csend, crecv, (sibling, row))
+
     def high_low(v):
         high = v.astype(BF16).astype(F32)
         return [high, (v - high).astype(BF16).astype(F32)]
@@ -308,44 +312,45 @@
     rows = [v[0:8] * (v[8:9] + v[9:10]) for v in blocks] + [square, jnp.zeros((8, 128), F32)]
     r4[row] = jnp.concatenate(rows, axis=0).astype(BF16)
     for to in row_peers:
-        send(r4.at[row], r4.at[row], ssem.at[4], rsem.at[4], (head, to))
+        send(r4.at[row], r4.at[row], ssem.at[4], rowsem.at[row], (head, to))
     arrived(r3.at[0:3], ssem.at[3])
 
-    arrived(wo.at[core], wrecv)
-    sibling = head + 1 - 2 * core
-    send(wo.at[core], wo.at[core], csend, crecv, (sibling, row))
-
+    which_row = lax.div(iota((1, 128), 1), 32)
+    arrived(wo.at[1 - core], crecv)
+
+    def onward(peers):
+        rows = []
+        for peer in peers:
+            block = r4[peer].astype(F32)
+            rows.append(jnp.concatenate([block[n * 8 : n * 8 + 8] for n in range(4)], axis=1))
+            for p in range(2):
+                square = block[32 + p * 4 : 33 + p * 4]
+                for n in range(1, 4):
+                    square = jnp.where(which_row == n, block[32 + p * 4 + n : 33 + p * 4 + n], square)
+                sq[2 * peer + p] = square
+        left_side = jnp.concatenate(rows, axis=0).astype(BF16)
+        outs = [dot(left_side, wo[n]) for n in range(2)]
+        for b, peer in enumerate(peers):
+            for p in range(2):
+                to = 2 * peer + p
+                for k in range(4):
+                    at = b * 8 + p * 4
+                    f5[to, pl.ds(k, 4, stride=4), :] = outs[k // 2][at : at + 4, k % 2 * 128 : k % 2 * 128 + 128]
+                s5[to] = f5[to].astype(BF16)
+
+                @pl.when(to != quad)
+                def _():
+                    send(sq.at[to], rq.at[quad], qsend, qrecv, (to * 4 + place, row))
+                    send(s5.at[to], r5.at[quad], xsend, xrecv, (to * 4 + place, row))
+
+    onward([row])
     for r in range(8, 16):
         update(r)
-
-    arrived(r4.at[0:7], rsem.at[4])
-    f4[...] = r4[...].reshape(384, 128).astype(F32)
-    which_row = lax.div(iota((8, 128), 1), 32)
-    for p in range(2):
-        square = f4[pl.ds(32 + p * 4, 8, stride=48), :]
-        for n in range(1, 4):
-            square = jnp.where(which_row == n, f4[pl.ds(32 + p * 4 + n, 8, stride=48), :], square)
-        for i in range(8):
-            sq[2 * i + p] = square[i : i + 1]
-    for d in (4, 12, 3, 5, 11, 13, 2, 6, 10, 14, 1, 7, 9, 15, 8):
-        to = lax.rem(quad + d, 16)
-        send(sq.at[to], rq.at[quad], qsend, qrecv, (to * 4 + place, row))
+    for peers in (row_peers[5:7], row_peers[3:5], row_peers[1:3], row_peers[0:1]):
+        for peer in peers:
+            arrived(r4.at[peer], rowsem.at[peer])
+        onward(peers)
     rq[quad] = sq[quad]
-    for n in range(4):
-        block = [f4[pl.ds(n * 8 + k, 8, stride=48), :] for k in range(8)]
-        lhs[:, n * 128 : n * 128 + 128] = jnp.concatenate(block, axis=0).astype(BF16)
-    arrived(wo.at[1 - core], crecv)
-    f5r = f5.reshape(256, 128)
-    for half in range(2):
-        out = dot(lhs[...], wo[half])
-        for n in range(8):
-            for k in range(2):
-                at = n // 4 * 16 + n % 4 * 4 + half * 2 + k
-                f5r[pl.ds(at, 8, stride=32), :] = out[n * 8 : n * 8 + 8, k * 128 : k * 128 + 128]
-    s5[...] = f5[...].astype(BF16)
-    for d in (4, 12, 3, 5, 11, 13, 2, 6, 10, 14, 1, 7, 9, 15, 8):
-        to = lax.rem(quad + d, 16)
-        send(s5.at[to], r5.at[quad], xsend, xrecv, (to * 4 + place, row))
     r5[quad] = s5[quad]
     arrived(r4.at[0:7], ssem.at[4])
     arrived(wo.at[core], csend)
@@ -461,8 +466,6 @@
             V((16, 1, 128), F32),
             V((2, 512, 256), BF16),
             V((32, 128), F32),
-            V((384, 128), F32),
-            V((64, 512), BF16),
             V((16, 16, 128), F32),
             V((128, 2048), BF16),
             dma((15,)),
@@ -478,6 +481,7 @@
             dma,
             dma,
             dma,
+            dma((8,)),
         ],
         compiler_params=pltpu.CompilerParams(
             collective_id=0, has_side_effects=True, vmem_limit_bytes=32 << 20

time: 41.5 us -> 39.8 us (0.959)
  the two profiles are of different devices: /device:TPU:1 before, /device:TPU:4 now
where the time goes in v5:
time: 39.8 us; the launch traced here: 39.7 us
  Pallas kernels  39.1 us (98%)
  between operations  0.65 us (2%)
    pallas_call x1, Pallas kernels, local(): pl.pallas_call(kernel, out_shape=(V((16, 16, 128), BF16), V((16, 1, 128),...  38 us
    pallas_call x1, Pallas kernels, local(): pl.pallas_call(hand_over, out_shape=shapes, in_specs=[vmem, vmem] + [pl.B...  1.03 us

profile of v5, /device:TPU:4, one launch (start us, length us, event | category | flops | bytes accessed | tf_op | source)
XLA Modules:
  0.0 39.7 jit_solution(18270057548537240414)
XLA Ops:
  0.6 38.0 %shard_map.183 = (bf16[16,16,128]{2,1,0:T(8,128)(2,1)S(1)}, f32[16,1,128]{2,1,0:T(1,128)S(1)}, f32[16,128,128]{2,1,0:T(8,128)S(1)}, bf16[3,16,128]{2,1,0:T(8,128)(2,1)S(1)}, bf16[3,16,32]{2,1,0:T(8,128)(2,1)S(1)}) custom-call(bf16[2,128,512]{2,1,0:T(8,128)(2,1)} %tokens_h.1, bf16[1024,128]{1,0:T(8,128)(2,1)} %bitcast.16, bf16[32,512]{1,0:T(8,128)(2,1)} %bitcast.17, ...), custom_call_target="tpu_custom_call" | custom-call | tf_op jit(solution)/shard_map/pallas_call | solution.py:429
  38.7 1.0 %shard_map.184 = (bf16[2,2,512]{2,1,0:T(2,128)(2,1)}, f32[16,128,128]{2,1,0:T(8,128)}, bf16[3,16,128]{2,1,0:T(8,128)(2,1)}, bf16[3,16,32]{2,1,0:T(8,128)(2,1)}) custom-call(bf16[16,16,128]{2,1,0:T(8,128)(2,1)S(1)} %get-tuple-element.13.parts, f32[16,1,128]{2,1,0:T(1,128)S(1)} %get-tuple-element.14.squares, f32[16,128,128]{2,1,0:T(8,128)S(1)} %get-tuple-element.15.a, ...), custom_call_target="tpu_custom_call" | custom-call | tf_op jit(solution)/shard_map/pallas_call | solution.py:490

commit v6 on v5

--- a/solution.py
+++ b/solution.py
@@ -241,6 +241,11 @@
     arrived(ra.at[0:7], ssem.at[0])
     arrived(rb.at[0:7], ssem.at[1])
     arrived(wo.at[0, 0:384, :], wsend)
+    s3[...] = jnp.zeros_like(s3)
+    s3r = s3.reshape(64, 128)
+    gain_high = norm_gain[...].astype(BF16).astype(F32)
+    s3r[pl.ds(8, 4, stride=16), :] = jnp.broadcast_to(gain_high, (4, 128))
+    s3r[pl.ds(9, 4, stride=16), :] = jnp.broadcast_to(norm_gain[...] - gain_high, (4, 128))
     arrived(rc, rsem.at[2])
     def channels(k):
         u = rc[k].astype(F32) + rc[k + 1].astype(F32)
@@ -262,14 +267,9 @@
     y1 = d01 * read[16:] + d1 * a0 * along(b0, c1) + a1 * along(b1, c1)
     gated = (jnp.concatenate([y0, y1], axis=0) + skip) * gate
     gs[...] = gated
-    s3[...] = jnp.zeros_like(s3)
-    s3r = s3.reshape(64, 128)
     for k in range(8):
         p, t, u = k // 4, k // 2 % 2, k % 2
         s3r[pl.ds(k, 4, stride=16), :] = gs[pl.ds(t * 16 + p * 8 + u, 4, stride=2), :]
-    gain_high = norm_gain[...].astype(BF16).astype(F32)
-    s3r[pl.ds(8, 4, stride=16), :] = jnp.broadcast_to(gain_high, (4, 128))
-    s3r[pl.ds(9, 4, stride=16), :] = jnp.broadcast_to(norm_gain[...] - gain_high, (4, 128))
     s3b[...] = s3[...].astype(BF16)
 
     for d in range(1, 4):
@@ -344,12 +344,12 @@
                     send(s5.at[to], r5.at[quad], xsend, xrecv, (to * 4 + place, row))
 
     onward([row])
-    for r in range(8, 16):
-        update(r)
     for peers in (row_peers[5:7], row_peers[3:5], row_peers[1:3], row_peers[0:1]):
         for peer in peers:
             arrived(r4.at[peer], rowsem.at[peer])
         onward(peers)
+    for r in range(8, 16):
+        update(r)
     rq[quad] = sq[quad]
     r5[quad] = s5[quad]
     arrived(r4.at[0:7], ssem.at[4])

time: 39.8 us -> 39.8 us (level)
  no operation moved by 1% of the time
where the time goes in v6:
time: 39.8 us; the launch traced here: 39.7 us
  Pallas kernels  39 us (98%)
  between operations  0.65 us (2%)
    pallas_call x1, Pallas kernels, local(): pl.pallas_call(kernel, out_shape=(V((16, 16, 128), BF16), V((16, 1, 128),...  38 us
    pallas_call x1, Pallas kernels, local(): pl.pallas_call(hand_over, out_shape=shapes, in_specs=[vmem, vmem] + [pl.B...  1.03 us

profile of v6, /device:TPU:4, one launch (start us, length us, event | category | flops | bytes accessed | tf_op | source)
XLA Modules:
  0.0 39.7 jit_solution(15759955001029767715)
XLA Ops:
  0.6 38.0 %shard_map.183 = (bf16[16,16,128]{2,1,0:T(8,128)(2,1)S(1)}, f32[16,1,128]{2,1,0:T(1,128)S(1)}, f32[16,128,128]{2,1,0:T(8,128)S(1)}, bf16[3,16,128]{2,1,0:T(8,128)(2,1)S(1)}, bf16[3,16,32]{2,1,0:T(8,128)(2,1)S(1)}) custom-call(bf16[2,128,512]{2,1,0:T(8,128)(2,1)} %tokens_h.1, bf16[1024,128]{1,0:T(8,128)(2,1)} %bitcast.16, bf16[32,512]{1,0:T(8,128)(2,1)} %bitcast.17, ...), custom_call_target="tpu_custom_call" | custom-call | tf_op jit(solution)/shard_map/pallas_call | solution.py:429
  38.7 1.0 %shard_map.184 = (bf16[2,2,512]{2,1,0:T(2,128)(2,1)}, f32[16,128,128]{2,1,0:T(8,128)}, bf16[3,16,128]{2,1,0:T(8,128)(2,1)}, bf16[3,16,32]{2,1,0:T(8,128)(2,1)}) custom-call(bf16[16,16,128]{2,1,0:T(8,128)(2,1)S(1)} %get-tuple-element.13.parts, f32[16,1,128]{2,1,0:T(1,128)S(1)} %get-tuple-element.14.squares, f32[16,128,128]{2,1,0:T(8,128)S(1)} %get-tuple-element.15.a, ...), custom_call_target="tpu_custom_call" | custom-call | tf_op jit(solution)/shard_map/pallas_call | solution.py:490
